TPU v7x, 32 devices: a whole 2x2x4 slice. The times are simulated.
32 devices in a mesh: dp: 16 (over z, y, x), tensor: 2 (over core).
Axes of the slice: x: 2, y: 2, z: 4, core: 2. Of those that a mesh axis runs over, the one named last changes fastest.
Arguments:
- inputs: bfloat16 [4096, 768], P('dp'), may hold values from -6 to 6
- lengths: int32 [32], P('dp'), may hold values from 1 to 128, as said below
- w_qkv: bfloat16 [2, 3, 768, 768], P(None, None, None, 'tensor'), may hold values from -0.21875 to 0.21875
- w_out: bfloat16 [2, 768, 768], P(None, 'tensor'), may hold values from -0.875 to 0.875
- w_in: bfloat16 [2, 2, 768, 3072], P(None, None, None, 'tensor'), may hold values from -0.21875 to 0.21875
- w_down: bfloat16 [2, 3072, 768], P(None, 'tensor'), may hold values from -0.15625 to 0.15625
- norm_gain: float32 [2, 2, 768], replicated, may hold values from 0.5 to 1.5
- norm_bias: float32 [2, 2, 768], replicated, may hold values from -3 to 3
- cotangent: bfloat16 [4096, 768], P('dp'), may hold values from -6 to 6
Outputs:
- encoded: bfloat16 [4096, 768], P('dp')
- input_grad: float32 [4096, 768], P('dp')
- grad_w_qkv: float32 [2, 3, 768, 768], P(None, None, 'dp', 'tensor')
- grad_w_out: float32 [2, 768, 768], P(None, 'tensor', 'dp')
- grad_w_in: float32 [2, 2, 768, 3072], P(None, None, 'dp', 'tensor')
- grad_w_down: float32 [2, 3072, 768], P(None, 'tensor', 'dp')
- grad_norm_gain: float32 [2, 2, 768], P(None, None, 'dp')
- grad_norm_bias: float32 [2, 2, 768], P(None, None, 'dp')
Inputs may be any that keep to these rules, and one draw needn't show every extreme that they name: `lengths`: among each run of 2 windows that starts at a multiple of 2, at least one has all 128 slots live.
All inputs are finite; a program needn't handle non-finite values.
Results may differ from a plain program's by a relative error of at most 0.025.
Values sent between devices are 32-bit elements; how exact they have to be, the bound alone decides.
A program may use at most 192 MiB of HBM per device.

v0:
```python
import jax
import jax.numpy as jnp
from jax import lax
from jax.sharding import PartitionSpec as P

HEADS = 12
HEAD_DIM = 64


EPS = 1e-05
MASKED = -1000000000.0


def normalize(values, gain_vec, shift_vec):
    center = values - jnp.mean(values, -1, keepdims=True)
    spread = jnp.mean(center * center, -1, keepdims=True)
    return center * lax.rsqrt(spread + EPS) * gain_vec + shift_vec


def gating(gate_pre, up_pre):
    return jax.nn.gelu(gate_pre, approximate=False) * up_pre


def head_bias(heads_local, length):
    first_head = lax.axis_index("tensor") * heads_local
    head_order = (first_head + jnp.arange(heads_local, dtype=jnp.int32)).astype(jnp.float32)
    slopes = 2.0 ** (-8.0 * (head_order + 1.0) / HEADS)
    places = jnp.arange(length, dtype=jnp.int32)
    distance = jnp.abs(places[:, None] - places[None, :]).astype(jnp.float32)
    return -slopes[:, None, None] * distance


def scores_of(query_heads, key_heads, bias_table, key_live):
    score_scale = query_heads.shape[-1] ** (-0.5)
    raw_scores = (
        jnp.einsum("wqhe,wkhe->whqk", query_heads, key_heads, preferred_element_type=jnp.float32)
        * score_scale
        + bias_table[None]
    )
    return jnp.where(key_live[:, None, None, :], raw_scores, MASKED)


def layer_forward(layer_rows, params, bias_table, key_live):
    qkv_weight, out_weight, in_weight, down_weight, gains_now, shifts_now = params
    windows, length = key_live.shape
    heads_local = bias_table.shape[0]
    rows_low = layer_rows.astype(jnp.bfloat16)
    projected = jnp.einsum(
        "td,cde->cte", rows_low, qkv_weight, preferred_element_type=jnp.float32
    ).astype(jnp.bfloat16)
    heads_split = projected.reshape(3, windows, length, heads_local, HEAD_DIM)
    scores = scores_of(heads_split[0], heads_split[1], bias_table, key_live)
    row_max = jnp.max(scores, -1, keepdims=True)
    log_total = row_max + jnp.log(jnp.sum(jnp.exp(scores - row_max), -1, keepdims=True))
    weights_low = jnp.exp(scores - log_total).astype(jnp.bfloat16)
    mixed_heads = jnp.einsum(
        "whqk,wkhe->wqhe", weights_low, heads_split[2], preferred_element_type=jnp.float32
    )
    mixed_heads = mixed_heads.astype(jnp.bfloat16).reshape(windows * length, heads_local * HEAD_DIM)
    attended = lax.psum(
        jnp.dot(mixed_heads, out_weight, preferred_element_type=jnp.float32), "tensor"
    )
    hidden = layer_rows + attended
    normed = normalize(hidden, gains_now[0], shifts_now[0])
    normed_low = normed.astype(jnp.bfloat16)
    gate_up = jnp.einsum("td,cdf->ctf", normed_low, in_weight, preferred_element_type=jnp.float32)
    gated_low = gating(gate_up[0], gate_up[1]).astype(jnp.bfloat16)
    fed_back = lax.psum(
        jnp.dot(gated_low, down_weight, preferred_element_type=jnp.float32), "tensor"
    )
    summed = normed + fed_back
    output = normalize(summed, gains_now[1], shifts_now[1])
    stored = (
        rows_low,
        projected,
        log_total,
        mixed_heads,
        hidden,
        normed_low,
        gate_up,
        gated_low,
        summed,
    )
    return (output, stored)


def layer_backward(grad_output, stored, params, bias_table, key_live):
    rows_low, projected, log_total, mixed_heads, hidden, normed_low, gate_up, gated_low, summed = (
        stored
    )
    qkv_weight, out_weight, in_weight, down_weight, gains_now, shifts_now = params
    windows, length = key_live.shape
    heads_local = bias_table.shape[0]
    _, pull_second = jax.vjp(normalize, summed, gains_now[1], shifts_now[1])
    grad_summed, gain_second, shift_second = pull_second(grad_output)
    grad_fed = grad_summed.astype(jnp.bfloat16)
    grad_gated = jnp.einsum("td,fd->tf", grad_fed, down_weight, preferred_element_type=jnp.float32)
    grad_down = jnp.einsum("tf,td->fd", gated_low, grad_fed, preferred_element_type=jnp.float32)
    _, pull_gate = jax.vjp(gating, gate_up[0], gate_up[1])
    grad_gate_pre, grad_up_pre = pull_gate(grad_gated)
    grad_gate_up = jnp.stack([grad_gate_pre, grad_up_pre]).astype(jnp.bfloat16)
    ffn_back = lax.psum(
        jnp.einsum("ctf,cdf->td", grad_gate_up, in_weight, preferred_element_type=jnp.float32),
        "tensor",
    )
    grad_in = jnp.einsum(
        "td,ctf->cdf", normed_low, grad_gate_up, preferred_element_type=jnp.float32
    )
    grad_normed = grad_summed + ffn_back
    _, pull_first = jax.vjp(normalize, hidden, gains_now[0], shifts_now[0])
    grad_hidden, gain_first, shift_first = pull_first(grad_normed)
    grad_attended = grad_hidden.astype(jnp.bfloat16)
    grad_mixed = jnp.einsum(
        "td,ed->te", grad_attended, out_weight, preferred_element_type=jnp.float32
    ).astype(jnp.bfloat16)
    grad_out_proj = jnp.einsum(
        "te,td->ed", mixed_heads, grad_attended, preferred_element_type=jnp.float32
    )
    heads_split = projected.reshape(3, windows, length, heads_local, HEAD_DIM)
    scores = scores_of(heads_split[0], heads_split[1], bias_table, key_live)
    probabilities = jnp.exp(scores - log_total)
    probs_low = probabilities.astype(jnp.bfloat16)
    grad_heads = grad_mixed.reshape(windows, length, heads_local, HEAD_DIM)
    grad_probs = jnp.einsum(
        "wqhe,wkhe->whqk", grad_heads, heads_split[2], preferred_element_type=jnp.float32
    )
    grad_values = jnp.einsum(
        "whqk,wqhe->wkhe", probs_low, grad_heads, preferred_element_type=jnp.float32
    )
    row_dot = jnp.sum(probabilities * grad_probs, -1, keepdims=True)
    grad_scores = (probabilities * (grad_probs - row_dot)).astype(jnp.bfloat16)
    score_scale = HEAD_DIM ** (-0.5)
    grad_query = (
        jnp.einsum(
            "whqk,wkhe->wqhe", grad_scores, heads_split[1], preferred_element_type=jnp.float32
        )
        * score_scale
    )
    grad_keys = (
        jnp.einsum(
            "whqk,wqhe->wkhe", grad_scores, heads_split[0], preferred_element_type=jnp.float32
        )
        * score_scale
    )
    grad_projected = jnp.stack([grad_query, grad_keys, grad_values]).astype(jnp.bfloat16)
    grad_projected = grad_projected.reshape(3, windows * length, heads_local * HEAD_DIM)
    attn_back = lax.psum(
        jnp.einsum("cte,cde->td", grad_projected, qkv_weight, preferred_element_type=jnp.float32),
        "tensor",
    )
    grad_qkv = jnp.einsum(
        "td,cte->cde", rows_low, grad_projected, preferred_element_type=jnp.float32
    )
    grad_rows = grad_hidden + attn_back
    grad_gains = jnp.stack([gain_first, gain_second])
    grad_shifts = jnp.stack([shift_first, shift_second])
    return (grad_rows, (grad_qkv, grad_out_proj, grad_in, grad_down, grad_gains, grad_shifts))


def body(inputs, lengths, w_qkv, w_out, w_in, w_down, norm_gain, norm_bias, cotangent):
    windows = lengths.shape[0]
    length = inputs.shape[0] // windows
    heads_local = w_qkv.shape[-1] // HEAD_DIM
    bias_table = head_bias(heads_local, length)
    key_live = jnp.arange(length, dtype=jnp.int32)[None, :] < lengths[:, None]
    layers = w_qkv.shape[0]
    layer_rows = inputs.astype(jnp.float32)
    stored_all = []
    for layer_index in range(layers):
        params = (
            w_qkv[layer_index],
            w_out[layer_index],
            w_in[layer_index],
            w_down[layer_index],
            norm_gain[layer_index],
            norm_bias[layer_index],
        )
        layer_rows, stored = layer_forward(layer_rows, params, bias_table, key_live)
        stored_all.append(stored)
    encoded = layer_rows.astype(jnp.bfloat16)
    grad_rows = cotangent.astype(jnp.float32)
    pieces = [None] * layers
    for layer_index in reversed(range(layers)):
        params = (
            w_qkv[layer_index],
            w_out[layer_index],
            w_in[layer_index],
            w_down[layer_index],
            norm_gain[layer_index],
            norm_bias[layer_index],
        )
        grad_rows, layer_grads = layer_backward(
            grad_rows, stored_all[layer_index], params, bias_table, key_live
        )
        pieces[layer_index] = layer_grads
    stacked = [jnp.stack([pieces[index][member] for index in range(layers)]) for member in range(6)]
    stacked = (
        lax.psum_scatter(stacked[0], "dp", scatter_dimension=2, tiled=True),
        lax.psum_scatter(stacked[1], "dp", scatter_dimension=2, tiled=True),
        lax.psum_scatter(stacked[2], "dp", scatter_dimension=2, tiled=True),
        lax.psum_scatter(stacked[3], "dp", scatter_dimension=2, tiled=True),
        lax.psum_scatter(stacked[4], "dp", scatter_dimension=2, tiled=True),
        lax.psum_scatter(stacked[5], "dp", scatter_dimension=2, tiled=True),
    )
    return (
        encoded,
        grad_rows,
        stacked[0],
        stacked[1],
        stacked[2],
        stacked[3],
        stacked[4],
        stacked[5],
    )


def solution(mesh):
    return jax.shard_map(
        body,
        mesh=mesh,
        in_specs=(
            P("dp", None),
            P("dp"),
            P(None, None, None, "tensor"),
            P(None, "tensor", None),
            P(None, None, None, "tensor"),
            P(None, "tensor", None),
            P(),
            P(),
            P("dp", None),
        ),
        out_specs=(
            P("dp", None),
            P("dp", None),
            P(None, None, "dp", "tensor"),
            P(None, "tensor", "dp"),
            P(None, None, "dp", "tensor"),
            P(None, "tensor", "dp"),
            P(None, None, "dp"),
            P(None, None, "dp"),
        ),
        check_vma=False,
    )
```

profile of v0, /device:TPU:0, one launch (start us, length us, event | category | flops | bytes accessed | tf_op | source)
XLA Modules:
  0.0 1569.1 jit_solution(8014279557188641523)
XLA Ops:
  8.0 2.2 fusion.126
  12.2 1.3 fusion.228
  14.2 21.3 %all-reduce.16.cloned.1.call-done = f32[256,768]{1,0:T(8,128)} async-done(((f32[256,768]{1,0:T(8,128)}), f32[256,768]{1,0:T(8,128)}) %all-reduce.16.cloned.1.call-update) | async-done | bytes 786448 | tf_op jit(solution)/shard_map/psum | solution.py:60
  35.5 1.3 fusion.361
  37.1 3.9 fusion.12
  41.1 1.6 copy-done.5
  42.7 4.9 fusion.24
  47.7 20.5 %all-reduce.18.cloned.1.call-done = f32[256,768]{1,0:T(8,128)} async-done(((f32[256,768]{1,0:T(8,128)}), f32[256,768]{1,0:T(8,128)}) %all-reduce.18.cloned.1.call-update) | async-done | bytes 786448 | tf_op jit(solution)/shard_map/psum | solution.py:68
  68.2 1.4 fusion.359
  70.5 2.3 fusion.129
  75.2 1.3 fusion.225
  76.8 20.3 %all-reduce.20.cloned.1.call-done = f32[256,768]{1,0:T(8,128)} async-done(((f32[256,768]{1,0:T(8,128)}), f32[256,768]{1,0:T(8,128)}) %all-reduce.20.cloned.1.call-update) | async-done | bytes 786448 | tf_op jit(solution)/shard_map/psum | solution.py:60
  97.0 1.8 fusion.357
  99.2 3.8 fusion.15
  103.0 1.7 copy-done.7
  104.7 4.9 fusion.20
  109.7 20.5 %all-reduce.22.cloned.1.call-done = f32[256,768]{1,0:T(8,128)} async-done(((f32[256,768]{1,0:T(8,128)}), f32[256,768]{1,0:T(8,128)}) %all-reduce.22.cloned.1.call-update) | async-done | bytes 786448 | tf_op jit(solution)/shard_map/psum | solution.py:68
  130.2 1.5 fusion.355
  134.0 2.8 fusion.18
  136.9 3.7 fusion.214
  142.8 4.6 fusion.113
  147.9 20.1 %all-reduce.24.cloned.1.call-done = f32[256,768]{1,0:T(8,128)} async-done(((f32[256,768]{1,0:T(8,128)}), f32[256,768]{1,0:T(8,128)}) %all-reduce.24.cloned.1.call-update) | async-done | bytes 786448 | tf_op jit(solution)/shard_map/psum | solution.py:102
  168.0 2.4 multiply_reduce_fusion
  172.8 1.7 copy.118
  174.5 1.7 reshape.292
  176.2 1.3 fusion.142
  177.5 1.3 multiply_reduce_fusion.6
  182.8 3.3 fusion.116
  186.3 20.5 %all-reduce.26.cloned.1.call-done = f32[256,768]{1,0:T(8,128)} async-done(((f32[256,768]{1,0:T(8,128)}), f32[256,768]{1,0:T(8,128)}) %all-reduce.26.cloned.1.call-update) | async-done | bytes 786448 | tf_op jit(solution)/shard_map/psum | solution.py:147
  206.8 1.8 multiply_reduce_fusion.1
  209.0 2.8 fusion.22
  211.9 3.7 fusion.215
  217.7 4.6 fusion.110
  222.7 5.8 convolution_bitcast_fusion.2
  230.9 12.0 all-reduce.28.cloned.1.call-done
  242.9 2.4 multiply_reduce_fusion.2
  247.7 1.7 copy.133
  249.4 1.7 reshape.293
  251.0 2.0 fusion.143
  253.0 1.3 multiply_reduce_fusion.3
  259.0 1.2 reshape.312
  267.0 3.3 fusion.119
  270.4 3.3 convolution_bitcast_fusion.3
  273.7 6.6 pad_maximum_fusion.1
  280.4 15.0 copy.156
  296.0 3.0 convolution_bitcast_fusion
  299.1 1.4 convolution_bitcast_fusion.6
  300.6 2.6 convolution_bitcast_fusion.4
  303.2 1.6 convolution_bitcast_fusion.1
  304.8 6.9 pad_maximum_fusion
  311.7 28.5 %copy.155 = f32[2,2,768,1536]{3,1,0,2:T(2,128)} copy(f32[2,2,768,1536]{2,3,1,0:T(8,128)} %pad_maximum_fusion) | data formatting | bytes 37748736 | tf_op jit(solution)/shard_map/stack | solution.py:196
  341.5 1.5 pad_maximum_fusion.3
  343.0 5.4 copy.152
  349.1 1.3 copy-done.2
  350.4 3.4 pad_maximum_fusion.2
  353.8 13.6 copy.151
  369.3 13.5 reduce-scatter.9.cloned.1.call-done
  384.3 124.2 %reduce-scatter.7.cloned.1.call-done = f32[48,4]{1,0:T(8,128)} async-done(((f32[768,4]{1,0:T(8,128)}), f32[48,4]{1,0:T(8,128)}) %reduce-scatter.7.cloned.1.call-update) | async-done | bytes 784
  510.1 19.7 %all-reduce.30.cloned.1.call-done = f32[256,768]{1,0:T(8,128)} async-done(((f32[256,768]{1,0:T(8,128)}), f32[256,768]{1,0:T(8,128)}) %all-reduce.30.cloned.1.call-update) | async-done | bytes 786448 | tf_op jit(solution)/shard_map/psum | solution.py:147
  529.7 2.2 add_add_fusion.4
  531.9 285.7 %all-reduce.32.cloned.1.call-done = f32[2,1536,768]{1,0,2:T(2,128)} async-done(((f32[2,1536,768]{1,0,2:T(2,128)}), f32[2,1536,768]{1,0,2:T(2,128)}) %all-reduce.32.cloned.1.call-update) | async-done | bytes 9437200
  819.7 736.0 %all-reduce.34.cloned.1.call-done = (f32[2,3,768,384]{3,0,1,2:T(2,128)}, f32[2,384,768]{1,0,2:T(2,128)}, f32[2,2,768,1536]{3,1,0,2:T(2,128)}) async-done(((f32[2,3,768,384]{3,0,1,2:T(2,128)}, f32[2,384,768]{1,0,2:T(2,128)}, f32[2,2,768,1536]{3,1,0,2:T(2,128)}), (f32[2,3,768,384]{3,0,1,2:T(2,128)}, f32[2,384,768]{1,0,2:T(2,128)}, f32[2,2,768,1536]{3,1,0,2:T(2,128)})) %all-reduce.34.cloned.1.call-update) | async-done | bytes 28311568
  1558.6 1.4 constant_dynamic-slice_fusion.1
  1559.9 1.4 copy.159
  (358 shorter events, 49.8 us)
Async XLA Ops:
  7.2 28.4 %all-reduce.16.cloned.1.call-start = ((), (), s32[]{:S(2)}) async-start(), calls=%async_computation.2 | async-start | bytes 1572864 | tf_op jit(solution)/shard_map/psum | solution.py:60
  11.4 24.2 %copy-start.41 = (bf16[256,768]{1,0:T(8,128)(2,1)S(1)}, bf16[256,768]{1,0:T(8,128)(2,1)}, u32[]{:S(2)}) copy-start(bf16[256,768]{1,0:T(8,128)(2,1)} %param.9) | copy-start | bytes 1179652
  13.5 54.8 %all-reduce.18.cloned.1.call-start = ((), (), s32[]{:S(2)}) async-start(), calls=%async_computation.3 | async-start | bytes 1572864 | tf_op jit(solution)/shard_map/psum | solution.py:68
  14.2 54.0 %copy-start.53 = (f32[768]{0:T(1024)}, f32[768]{0:T(1024)S(1)}, u32[]{:S(2)}) copy-start(f32[768]{0:T(1024)S(1)} %get-tuple-element.94) | copy-start | bytes 9220
  14.2 54.0 %copy-start.69 = (f32[768]{0:T(1024)}, f32[768]{0:T(1024)S(1)}, u32[]{:S(2)}) copy-start(f32[768]{0:T(1024)S(1)} %get-tuple-element.50) | copy-start | bytes 9220
  14.2 55.8 %copy-start.55 = (f32[768]{0:T(1024)}, f32[768]{0:T(1024)S(1)}, u32[]{:S(2)}) copy-start(f32[768]{0:T(1024)S(1)} %get-tuple-element.95) | copy-start | bytes 9220
  14.2 55.8 %copy-start.71 = (f32[768]{0:T(1024)}, f32[768]{0:T(1024)S(1)}, u32[]{:S(2)}) copy-start(f32[768]{0:T(1024)S(1)} %get-tuple-element.49) | copy-start | bytes 9220
  36.8 31.4 %copy-start.60 = (f32[256]{0:T(256)}, f32[256]{0:T(256)S(1)}, u32[]{:S(2)}) copy-start(f32[256]{0:T(256)S(1)} %broadcast_multiply_fusion.4) | copy-start | bytes 3076
  36.8 5.9 slice-start
  37.1 4.0 copy-start.104
  37.1 31.1 %copy-start.76 = (f32[256]{0:T(256)}, f32[256]{0:T(256)S(1)}, u32[]{:S(2)}) copy-start(f32[256]{0:T(256)S(1)} %fusion.269) | copy-start | bytes 3076
  37.1 5.6 slice-start.1
  47.7 49.3 %all-reduce.20.cloned.1.call-start = ((), (), s32[]{:S(2)}) async-start(), calls=%async_computation.4 | async-start | bytes 1572864 | tf_op jit(solution)/shard_map/psum | solution.py:60
  74.3 22.7 %copy-start.56 = (f32[768]{0:T(1024)S(1)}, f32[768]{0:T(1024)}, u32[]{:S(2)}) copy-start(f32[768]{0:T(1024)} %copy-done.55) | copy-start | bytes 9220
  74.3 22.7 %copy-start.64 = (f32[256]{0:T(256)S(1)}, f32[256]{0:T(256)}, u32[]{:S(2)}) copy-start(f32[256]{0:T(256)} %copy-done.63) | copy-start | bytes 3076
  74.4 22.7 %copy-start.72 = (f32[768]{0:T(1024)S(1)}, f32[768]{0:T(1024)}, u32[]{:S(2)}) copy-start(f32[768]{0:T(1024)} %copy-done.71) | copy-start | bytes 9220
  74.4 22.7 %copy-start.80 = (f32[256]{0:T(256)S(1)}, f32[256]{0:T(256)}, u32[]{:S(2)}) copy-start(f32[256]{0:T(256)} %copy-done.79) | copy-start | bytes 3076
  76.5 22.7 %copy-start.58 = (f32[768]{0:T(1024)S(1)}, f32[768]{0:T(1024)}, u32[]{:S(2)}) copy-start(f32[768]{0:T(1024)} %get-tuple-element.93) | copy-start | bytes 9220
  76.5 22.7 %copy-start.74 = (f32[768]{0:T(1024)S(1)}, f32[768]{0:T(1024)}, u32[]{:S(2)}) copy-start(f32[768]{0:T(1024)} %get-tuple-element.51) | copy-start | bytes 9220
  76.5 53.7 %all-reduce.22.cloned.1.call-start = ((), (), s32[]{:S(2)}) async-start(), calls=%async_computation.5 | async-start | bytes 1572864 | tf_op jit(solution)/shard_map/psum | solution.py:68
  97.0 7.7 slice-start.2
  98.9 71.5 %copy-start.67 = (f32[256]{0:T(256)}, f32[256]{0:T(256)S(1)}, u32[]{:S(2)}) copy-start(f32[256]{0:T(256)S(1)} %broadcast_multiply_fusion.2) | copy-start | bytes 3076
  99.1 71.3 %copy-start.83 = (f32[256]{0:T(256)}, f32[256]{0:T(256)S(1)}, u32[]{:S(2)}) copy-start(f32[256]{0:T(256)S(1)} %fusion.271) | copy-start | bytes 3076
  99.2 5.6 slice-start.3
  109.7 22.3 %copy-start.75 = (f32[768]{0:T(1024)S(1)}, f32[768]{0:T(1024)}, u32[]{:S(2)}) copy-start(f32[768]{0:T(1024)} %get-tuple-element.96) | copy-start | bytes 9220
  109.7 58.3 %all-reduce.24.cloned.1.call-start = ((), (), s32[]{:S(2)}) async-start(), calls=%async_computation.6 | async-start | bytes 1572864 | tf_op jit(solution)/shard_map/psum | solution.py:102
  134.0 34.0 %copy-start.88 = (f32[256]{0:T(256)}, f32[256]{0:T(256)S(1)}, u32[]{:S(2)}) copy-start(f32[256]{0:T(256)S(1)} %negate_multiply_fusion.5) | copy-start | bytes 3076
  147.5 59.3 %all-reduce.26.cloned.1.call-start = ((), (), s32[]{:S(2)}) async-start(), calls=%async_computation.7 | async-start | bytes 1572864 | tf_op jit(solution)/shard_map/psum | solution.py:147
  171.7 5.8 copy-start.40
  180.5 5.7 copy-start.44
  182.8 23.9 %copy-start.1 = (f32[256,768]{1,0:T(8,128)S(1)}, f32[256,768]{1,0:T(8,128)}, u32[]{:S(2)}) copy-start(f32[256,768]{1,0:T(8,128)} %copy-done) | copy-start | bytes 2359300
  182.8 23.9 %copy-start.57 = (f32[768]{0:T(1024)S(1)}, f32[768]{0:T(1024)}, u32[]{:S(2)}) copy-start(f32[768]{0:T(1024)} %copy-done.55) | copy-start | bytes 9220
  182.8 23.9 %copy-start.65 = (f32[256]{0:T(256)S(1)}, f32[256]{0:T(256)}, u32[]{:S(2)}) copy-start(f32[256]{0:T(256)} %copy-done.63) | copy-start | bytes 3076
  186.2 22.4 %copy-start.107 = (f32[256]{0:T(256)S(1)}, f32[256]{0:T(256)}, u32[]{:S(2)}) copy-start(f32[256]{0:T(256)} %copy-done.106) | copy-start | bytes 3076
  186.2 22.4 %copy-start.81 = (f32[256]{0:T(256)S(1)}, f32[256]{0:T(256)}, u32[]{:S(2)}) copy-start(f32[256]{0:T(256)} %copy-done.79) | copy-start | bytes 3076
  186.2 56.7 %all-reduce.28.cloned.1.call-start = ((), (), s32[]{:S(2)}) async-start(), calls=%async_computation.8 | async-start | bytes 1572864 | tf_op jit(solution)/shard_map/psum | solution.py:102
  209.0 33.9 %copy-start.86 = (f32[256]{0:T(256)}, f32[256]{0:T(256)S(1)}, u32[]{:S(2)}) copy-start(f32[256]{0:T(256)S(1)} %negate_multiply_fusion.3) | copy-start | bytes 3076
  217.7 4.9 copy-start.92
  217.7 4.9 copy-start.91
  217.7 4.9 copy-start.89
  222.3 160.5 %reduce-scatter.9.cloned.1.call-start = ((), (), s32[]{:S(2)}) async-start(), calls=%async_computation.11 | async-start | bytes 417792
  222.6 5.8 copy-start.94
  222.6 5.8 copy-start.93
  222.6 20.3 %copy-start.54 = (f32[768]{0:T(1024)S(1)}, f32[768]{0:T(1024)}, u32[]{:S(2)}) copy-start(f32[768]{0:T(1024)} %copy-done.53) | copy-start | bytes 9220
  222.6 20.3 %copy-start.61 = (f32[256]{0:T(256)S(1)}, f32[256]{0:T(256)}, u32[]{:S(2)}) copy-start(f32[256]{0:T(256)} %copy-done.60) | copy-start | bytes 3076
  222.7 20.2 %copy-start.77 = (f32[256]{0:T(256)S(1)}, f32[256]{0:T(256)}, u32[]{:S(2)}) copy-start(f32[256]{0:T(256)} %copy-done.76) | copy-start | bytes 3076
  230.9 14.4 copy-start.105
  246.6 6.5 copy-start.38
  255.6 5.4 copy-start.84
  255.6 6.0 copy-start.50
  260.2 3.2 copy-start.51
  260.2 248.4 %reduce-scatter.7.cloned.1.call-start = ((), (), s32[]{:S(2)}) async-start(), calls=%async_computation.10 | async-start | bytes 417792
  266.9 3.5 copy-start.10
  266.9 3.5 copy-start.87
  266.9 262.8 %all-reduce.30.cloned.1.call-start = ((), (), s32[]{:S(2)}) async-start(), calls=%async_computation.9 | async-start | bytes 1572864 | tf_op jit(solution)/shard_map/psum | solution.py:147
  270.3 547.3 %all-reduce.32.cloned.1.call-start = ((), (), s32[]{:S(2)}) async-start(), calls=%async_computation.12 | async-start | bytes 18874368
  295.4 3.6 copy-start.13
  295.4 1260.3 %all-reduce.34.cloned.1.call-start = ((), (), s32[]{:S(2)}) async-start(), calls=%async_computation.13 | async-start | bytes 56623104
  311.7 28.5 %copy-start.15 = (f32[256,768]{1,0:T(8,128)S(1)}, f32[256,768]{1,0:T(8,128)}, u32[]{:S(2)}) copy-start(f32[256,768]{1,0:T(8,128)} %copy-done.14) | copy-start | bytes 2359300
  311.7 28.5 %copy-start.36 = (bf16[2,128,6,64]{1,0,3,2:T(2,128)(2,1)S(1)}, bf16[2,128,6,64]{1,0,3,2:T(2,128)(2,1)}, u32[]{:S(2)}) copy-start(bf16[2,128,6,64]{1,0,3,2:T(2,128)(2,1)} %copy-done.35) | copy-start | bytes 589828
  311.7 28.5 %copy-start.100 = (f32[256]{0:T(256)S(1)}, f32[256]{0:T(256)}, u32[]{:S(2)}) copy-start(f32[256]{0:T(256)} %copy-done.99) | copy-start | bytes 3076
  343.0 5.4 copy-start.42
  343.0 5.4 copy-start.48
  343.0 5.4 copy-start.49
  (61 other events, 98.1 us)
Sparse Core Ops, SparseCore 0:
  13.6 21.9 all-reduce.15
  47.8 20.3 all-reduce.17
  76.6 20.3 all-reduce.19
  109.8 20.3 all-reduce.21
  147.6 20.3 all-reduce.23
  186.3 20.3 all-reduce.25
  222.5 20.3 all-reduce.27
  260.3 122.4 reduce-scatter.8
  388.1 120.4 reduce-scatter.6
  511.4 18.2 all-reduce.29
  535.9 281.7 all-reduce.31
  823.9 731.6 all-reduce.33
where the time goes:
time: 1580 us; the launch traced here: 1570 us
  waiting for transfers between devices  1310 us (83%)
  local copies, waits for them, and re-layouts  109 us (7%)
  matrix products  76.8 us (5%)
  other arithmetic  50.4 us (3%)
  between operations  16.7 us (1%)
    unnamed x16, waiting for transfers between devices  1160 us
    another operation x4, local copies, waits for them, and re-layouts, body(): jnp.stack([pieces[index][member] for index in range(layers)])  62.5 us
    psum x2, waiting for transfers between devices, layer_forward(): lax.psum(jnp.dot(mixed_heads, out_weight, preferred_element_type=jnp.floa...  41.6 us
    psum x2, waiting for transfers between devices, layer_forward(): lax.psum(jnp.dot(gated_low, down_weight, preferred_element_type=jnp.float...  41 us
    psum x2, waiting for transfers between devices, layer_backward(): lax.psum(jnp.einsum('cte,cde->td', grad_projected, qkv_weight, preferred_...  40.2 us
    psum x2, waiting for transfers between devices, layer_backward(): lax.psum(jnp.einsum('ctf,cdf->td', grad_gate_up, in_weight, preferred_ele...  32.1 us
  transfers between devices with their start and end apart: 12, of which 12 were waited for; matrix products, arithmetic and copies ran while one was open for 8% of the time, Pallas kernels for 0%

commit v1 on v0

--- a/solution.py
+++ b/solution.py
@@ -1,14 +1,606 @@
+import functools
+
 import jax
 import jax.numpy as jnp
 from jax import lax
+from jax.experimental import pallas as pl
+from jax.experimental.pallas import tpu as pltpu
 from jax.sharding import PartitionSpec as P
 
 HEADS = 12
 HEAD_DIM = 64
-
-
 EPS = 1e-05
 MASKED = -1000000000.0
+MESH = pl.DeviceIdType.MESH
+F32 = jnp.float32
+BF16 = jnp.bfloat16
+PLANE = 4
+DP = 16
+
+
+def dot(a, b):
+    return lax.dot_general(a, b, (((1,), (0,)), ((), ())), preferred_element_type=F32)
+
+
+def dot_t(a, b):
+    return lax.dot_general(a, b, (((1,), (1,)), ((), ())), preferred_element_type=F32)
+
+
+def dot_tt(a, b):
+    return lax.dot_general(a, b, (((0,), (0,)), ((), ())), preferred_element_type=F32)
+
+
+def gelu_parts(g):
+    bell = jnp.exp(-0.5 * g * g)
+    d = 1.0 + (0.3275911 * 0.7071067811865476) * jnp.abs(g)
+    t = pl.reciprocal(d, approx=True)
+    t = t * (2.0 - d * t)
+    poly = t * (0.127414796 + t * (-0.142248368 + t * (0.7107068705 + t * (-0.7265760135 + t * 0.5307027145))))
+    tail = poly * bell
+    phi = jnp.where(g >= 0, 1.0 - tail, tail)
+    return g * phi, phi + g * (bell * 0.3989422804014327)
+
+
+def kernel(
+    T, D, E, F, L,
+    len_ref, x_ref, cot_ref, gain_ref, bias_ref, wq_hbm, wo_hbm, wi_hbm, wd_hbm,
+    enc_ref, igrad_ref, oatt, offn, gn, ag,
+    wq, wo, wi, wd, xb, qkv, pb, om, hhat, zhat, hr, zr, xcur, acur, ab, psend, precv, eb, AB, dob, dqkv, xbT, dabT,
+    abT, dfbT, edg, stage, GS, RZ1, RZ2, GA, RA1, RA2, RA3, RA4, gnr,
+    wsem, ps_s, ps_r, agl, ag_s, ag_r, stsem, fz_s, fz_r, fa_s, fa_r, fl, at_s, at_r, atl, gn_s, gn_r, cr_att, cr_ffn,
+):
+    dp = lax.axis_index("dp")
+    c = lax.axis_index("tensor")
+    q = lax.rem(dp, PLANE)
+    x = lax.rem(dp, 2)
+    y = lax.rem(lax.div(dp, 2), 2)
+    z0 = lax.rem(lax.div(dp, 4), 2)
+    z1 = lax.div(dp, 8)
+    nx, ny, nz0, nz1 = 1 - x, 1 - y, 1 - z0, 1 - z1
+    sib = (dp, 1 - c)
+    px = (dp + 1 - 2 * x, c)
+    py = (dp + 2 - 4 * y, c)
+    pxy = (dp + 3 - 2 * x - 4 * y, c)
+    pz0 = (dp + 4 - 8 * z0, c)
+    pz1 = (dp + 8 - 16 * z1, c)
+    W = T // 128
+    NP = E // 128
+    FQ = F // PLANE
+    NC = D // 256
+    R = D // DP
+    RB = D // (DP // PLANE)
+
+    barrier = pltpu.get_barrier_semaphore()
+    for peer in (sib, px, py, pxy, pz0, pz1):
+        pl.semaphore_signal(barrier, inc=1, device_id=peer, device_id_type=MESH)
+    pl.semaphore_wait(barrier, 6)
+
+    def remote(src, dst, ss, rs, peer):
+        return pltpu.make_async_remote_copy(
+            src_ref=src, dst_ref=dst, send_sem=ss, recv_sem=rs, device_id=peer, device_id_type=MESH
+        )
+
+    wcopies = {}
+    for l in range(L):
+        for i, (src, dst) in enumerate(((wq_hbm, wq), (wo_hbm, wo), (wi_hbm, wi), (wd_hbm, wd))):
+            cp = pltpu.make_async_copy(src.at[l], dst.at[l], wsem.at[l, i])
+            cp.start()
+            wcopies[l, i] = cp
+
+    RC = 64
+    row_chunks = [pl.ds(r, RC) for r in range(0, T, RC)]
+
+    def psum_send(slot, part):
+        cps = []
+        for n in range(NC):
+            psend[slot, n] = part(n)
+            cp = remote(psend.at[slot, n], precv.at[slot, n], ps_s.at[slot, n], ps_r.at[slot, n], sib)
+            cp.start()
+            cps.append(cp)
+        return cps
+
+    def psum_wait(cps):
+        for cp in cps:
+            cp.wait()
+
+    def psum_rows(slot, rows):
+        return jnp.concatenate([psend[slot, n, rows, :] + precv[slot, n, rows, :] for n in range(NC)], axis=1)
+
+    def norm_rows(v):
+        center = v - jnp.mean(v, -1, keepdims=True)
+        r = lax.rsqrt(jnp.mean(center * center, -1, keepdims=True) + EPS)
+        return center * r, r
+
+    def ln_bwd_rows(dy, hat, r, gain):
+        t = dy * gain
+        m1 = jnp.mean(t, -1, keepdims=True)
+        m2 = jnp.mean(t * hat, -1, keepdims=True)
+        return r * (t - m1 - hat * m2)
+
+    lane = lax.broadcasted_iota(jnp.int32, (128, 128), 1)
+    first = lane < HEAD_DIM
+
+    def halves(v):
+        zero = jnp.zeros_like(v)
+        return jnp.concatenate([jnp.where(first, v, zero), jnp.where(first, zero, v)], axis=0)
+
+    def ag_local(k):
+        cp = pltpu.make_async_copy(acur, ag.at[k, q], agl.at[k])
+        cp.start()
+        return cp
+
+    def ag_send(k, local):
+        local.wait()
+        cps = []
+        for j, peer in enumerate((px, py, pxy)):
+            cp = remote(ag.at[k, q], ag.at[k, q], ag_s.at[k, j], ag_r.at[k, j], peer)
+            cp.start()
+            cps.append(cp)
+        return cps
+
+    slope_table = [[2.0 ** (-8.0 * (cc * (E // HEAD_DIM) + h + 1.0) / HEADS) for h in range(E // HEAD_DIM)] for cc in range(HEADS * HEAD_DIM // E)]
+
+    def slope(h):
+        s = jnp.float32(slope_table[0][h])
+        for cc in range(1, len(slope_table)):
+            s = jnp.where(c == cc, jnp.float32(slope_table[cc][h]), s)
+        return s
+
+    def forward(l, src_rows):
+        for rows in row_chunks:
+            xb[l, rows, :] = src_rows(rows).astype(BF16)
+        wcopies[l, 0].wait()
+        for k in range(3):
+            qkv[l, k] = dot(xb[l], wq[l, k]).astype(BF16)
+        dist = jnp.abs(
+            lax.broadcasted_iota(jnp.int32, (128, 128), 0) - lane
+        ).astype(F32)
+
+        def attend(w, _):
+            rows = pl.ds(pl.multiple_of(w * 128, 128), 128)
+            live = lane < len_ref[w]
+            for p in range(NP):
+                cols = pl.ds(p * 128, 128)
+                kk = halves(qkv[l, 1, rows, cols])
+                vv = halves(qkv[l, 2, rows, cols])
+                s = dot_t(qkv[l, 0, rows, cols], kk)
+                both = []
+                for i in range(2):
+                    si = s[:, i * 128:(i + 1) * 128] * (HEAD_DIM ** -0.5) - slope(2 * p + i) * dist
+                    si = jnp.where(live, si, MASKED)
+                    ei = jnp.exp(si - jnp.max(si, -1, keepdims=True))
+                    both.append(ei / jnp.sum(ei, -1, keepdims=True))
+                prob = jnp.concatenate(both, axis=1).astype(BF16)
+                pb[l, w, p] = prob
+                om[l, rows, cols] = dot(prob, vv).astype(BF16)
+            return 0
+
+        lax.fori_loop(0, W, attend, 0)
+        wcopies[l, 1].wait()
+        cps = psum_send(0, lambda n: dot(om[l], wo[l, :, pl.ds(n * 256, 256)]))
+        wcopies[l, 2].wait()
+        psum_wait(cps)
+        gain, bias = gain_ref[l, 0:1, :], bias_ref[l, 0:1, :]
+        for rows in row_chunks:
+            hat, r = norm_rows(src_rows(rows) + psum_rows(0, rows))
+            hhat[l, rows, :] = hat.astype(BF16)
+            hr[l, rows, :] = r
+            a = hat * gain + bias
+            acur[rows, :] = a
+            ab[rows, :] = a.astype(BF16)
+        local = ag_local(l)
+
+        def hidden(j, _):
+            cols = pl.ds(pl.multiple_of(j * 256, 256), 256)
+            g = dot(ab[...], wi[l, 0, :, cols])
+            u = dot(ab[...], wi[l, 1, :, cols])
+            act, slope_g = gelu_parts(g)
+            eb[:, cols] = (act * u).astype(BF16)
+            AB[l, 0, :, cols] = act.astype(BF16)
+            AB[l, 1, :, cols] = (slope_g * u).astype(BF16)
+            return 0
+
+        lax.fori_loop(0, F // 256, hidden, 0)
+        sends = ag_send(l, local)
+        wcopies[l, 3].wait()
+        cps = psum_send(1, lambda n: dot(eb[...], wd[l, :, pl.ds(n * 256, 256)]))
+        psum_wait(cps)
+        gain, bias = gain_ref[l, 1:2, :], bias_ref[l, 1:2, :]
+        for rows in row_chunks:
+            hat, r = norm_rows(acur[rows, :] + psum_rows(1, rows))
+            zhat[l, rows, :] = hat.astype(BF16)
+            zr[l, rows, :] = r
+            out = hat * gain + bias
+            if l == L - 1:
+                enc_ref[rows, :] = out.astype(BF16)
+            else:
+                xcur[rows, :] = out
+        return sends
+
+    def bwd_norm2(l, src_rows):
+        gain = gain_ref[l, 1:2, :]
+        dg = jnp.zeros((1, D), F32)
+        db = jnp.zeros((1, D), F32)
+        for rows in row_chunks:
+            dy = src_rows(rows)
+            hat = zhat[l, rows, :].astype(F32)
+            dz = ln_bwd_rows(dy, hat, zr[l, rows, :], gain)
+            acur[rows, :] = dz
+            ab[rows, :] = dz.astype(BF16)
+            dg = dg + jnp.sum(dy * hat, 0, keepdims=True)
+            db = db + jnp.sum(dy, 0, keepdims=True)
+        gn[pl.ds(2 * l + 1, 1), :] = dg
+        gn[pl.ds(2 * L + 2 * l + 1, 1), :] = db
+
+    def bwd_hidden(l):
+        def hidden(j, _):
+            cols = pl.ds(pl.multiple_of(j * 256, 256), 256)
+            de = dot_t(ab[...], wd[l, cols, :])
+            dg = de * AB[l, 1, :, cols].astype(F32)
+            du = de * AB[l, 0, :, cols].astype(F32)
+            AB[l, 0, :, cols] = dg.astype(BF16)
+            AB[l, 1, :, cols] = du.astype(BF16)
+            return 0
+
+        lax.fori_loop(0, F // 256, hidden, 0)
+
+    def bwd_ffn_sum(l):
+        return psum_send(
+            0,
+            lambda n: dot_t(AB[l, 0], wi[l, 0, pl.ds(n * 256, 256), :]) + dot_t(AB[l, 1], wi[l, 1, pl.ds(n * 256, 256), :]),
+        )
+
+    def bwd_norm1(l):
+        gain = gain_ref[l, 0:1, :]
+        dg = jnp.zeros((1, D), F32)
+        db = jnp.zeros((1, D), F32)
+        for rows in row_chunks:
+            da = acur[rows, :] + psum_rows(0, rows)
+            hat = hhat[l, rows, :].astype(F32)
+            dh = ln_bwd_rows(da, hat, hr[l, rows, :], gain)
+            acur[rows, :] = dh
+            ab[rows, :] = dh.astype(BF16)
+            dg = dg + jnp.sum(da * hat, 0, keepdims=True)
+            db = db + jnp.sum(da, 0, keepdims=True)
+        gn[pl.ds(2 * l, 1), :] = dg
+        gn[pl.ds(2 * L + 2 * l, 1), :] = db
+
+    def bwd_attention(l):
+        dob[...] = dot_t(ab[...], wo[l]).astype(BF16)
+
+        def attend(w, _):
+            rows = pl.ds(pl.multiple_of(w * 128, 128), 128)
+            for p in range(NP):
+                cols = pl.ds(p * 128, 128)
+                qq = qkv[l, 0, rows, cols]
+                kk = halves(qkv[l, 1, rows, cols])
+                vv = halves(qkv[l, 2, rows, cols])
+                do = dob[rows, cols]
+                prob = pb[l, w, p]
+                dprob = dot_t(do, vv)
+                p32 = prob.astype(F32)
+                both = []
+                for i in range(2):
+                    pi, di = p32[:, i * 128:(i + 1) * 128], dprob[:, i * 128:(i + 1) * 128]
+                    both.append(pi * (di - jnp.sum(pi * di, -1, keepdims=True)))
+                ds = jnp.concatenate(both, axis=1).astype(BF16)
+                dv2 = dot_tt(prob, do)
+                dk2 = dot_tt(ds, qq)
+                scale = HEAD_DIM ** -0.5
+                dqkv[0, rows, cols] = (dot(ds, kk) * scale).astype(BF16)
+                dqkv[1, rows, cols] = (jnp.where(first, dk2[:128], dk2[128:]) * scale).astype(BF16)
+                dqkv[2, rows, cols] = jnp.where(first, dv2[:128], dv2[128:]).astype(BF16)
+            return 0
+
+        lax.fori_loop(0, W, attend, 0)
+
+    def bwd_qkv_sum(l):
+        return psum_send(
+            1,
+            lambda n: sum(dot_t(dqkv[k], wq[l, k, pl.ds(n * 256, 256), :]) for k in range(3)),
+        )
+
+    def att_views(k):
+        if k < 2:
+            return (
+                (GA.at[k, :, :, :, nx], GA.at[k, :, :, :, x], RA1.at[k], px),
+                (GA.at[k, :, :, ny, x], GA.at[k, :, :, y, x], RA2.at[k], py),
+                (GA.at[k, :, nz0, y, x], GA.at[k, :, z0, y, x], RA3.at[k], pz0),
+                (GA.at[k, nz1, z0, y, x], GA.at[k, z1, z0, y, x], RA4.at[k], pz1),
+            )
+        return (
+            (GA.at[k, :, :, ny], GA.at[k, :, :, y], RA1.at[k], py),
+            (GA.at[k, :, :, y, nx], GA.at[k, :, :, y, x], RA2.at[k], px),
+            (GA.at[k, :, nz0, y, x], GA.at[k, :, z0, y, x], RA3.at[k], pz0),
+            (GA.at[k, nz1, z0, y, x], GA.at[k, z1, z0, y, x], RA4.at[k], pz1),
+        )
+
+    att_cp = {}
+
+    def att_send(l, k, step):
+        src, _, dst, peer = att_views(k)[step]
+        if l < L - 1:
+            pl.semaphore_wait(cr_att.at[k, step], 1)
+        cp = remote(src, dst, at_s.at[k, step], at_r.at[k, step], peer)
+        cp.start()
+        att_cp[l, k, step] = cp
+
+    def att_recv(l, k, step):
+        _, keep, dst, peer = att_views(k)[step]
+        att_cp[l, k, step].wait_recv()
+        keep[...] = keep[...] + dst[...]
+        if l > 0:
+            pl.semaphore_signal(cr_att.at[k, step], inc=1, device_id=peer, device_id_type=MESH)
+        if step < 3:
+            att_send(l, k, step + 1)
+        else:
+            cp = pltpu.make_async_copy(GA.at[k, z1, z0, y, x], oatt.at[l, k], atl.at[k])
+            cp.start()
+            att_cp[l, k, "out"] = cp
+
+    def att_done(l, k):
+        for step in range(4):
+            att_cp[l, k, step].wait_send()
+        att_cp[l, k, "out"].wait()
+
+    def att_grad_prepare(l):
+        xbT[...] = xb[l].T
+        dabT[...] = ab[...].T
+
+    def att_grad(l, k):
+        left, right = (xbT, dqkv.at[k]) if k < 3 else (dabT, om.at[l])
+        for i in range(2):
+            half = D // 2
+            GA[k, i] = dot(left[pl.ds(i * half, half), :], right[...]).reshape(2, 2, 2, R, E)
+        att_send(l, k, 0)
+
+    def stage_copies(l, src, slot):
+        return (
+            pltpu.make_async_copy(ag.at[l, src], stage.at[slot, 0], stsem.at[slot, 0]),
+            pltpu.make_async_copy(ag.at[2 * L - 1 - l, src], stage.at[slot, 1], stsem.at[slot, 1]),
+        )
+
+    def ffn_hidden(l):
+        for cp in stage_copies(l, 0, 0):
+            cp.start()
+        qcols = pl.ds(pl.multiple_of(q * FQ, 128), FQ)
+
+        def chunk(s, _):
+            slot = lax.rem(s, 2)
+
+            @pl.when(s < PLANE - 1)
+            def _():
+                for cp in stage_copies(l, s + 1, 1 - slot):
+                    cp.start()
+
+            for cp in stage_copies(l, s, slot):
+                cp.wait()
+            toks = pl.ds(pl.multiple_of(s * T, T), T)
+            a = stage[slot, 0].astype(BF16)
+            dfb = stage[slot, 1].astype(BF16)
+            abT[:, toks] = a.T
+            dfbT[:, toks] = dfb.T
+            g = dot(a, wi[l, 0, :, qcols])
+            u = dot(a, wi[l, 1, :, qcols])
+            de = dot_t(dfb, wd[l, qcols, :])
+            act, slope_g = gelu_parts(g)
+            edg[toks, pl.ds(0, FQ)] = (de * u * slope_g).astype(BF16)
+            edg[toks, pl.ds(FQ, FQ)] = (de * act).astype(BF16)
+            edg[toks, pl.ds(2 * FQ, FQ)] = (act * u).astype(BF16)
+            return 0
+
+        lax.fori_loop(0, PLANE, chunk, 0)
+
+    ffn_cp = {}
+
+    def ffn_block(l, i):
+        b1, b0 = ((nz1, nz0), (z1, nz0), (nz1, z0), (z1, z0))[i]
+        rows = pl.ds(pl.multiple_of((b1 * 2 + b0) * RB, 64), RB)
+        for k in range(3):
+            left = abT if k < 2 else dfbT
+            GS[b1, b0, k] = dot(left[rows, :], edg[:, pl.ds(k * FQ, FQ)])
+        if i < 2:
+            if l < L - 1:
+                pl.semaphore_wait(cr_ffn.at[i], 1)
+            cp = remote(GS.at[b1, b0], RZ1.at[i], fz_s.at[i], fz_r.at[i], pz0)
+            cp.start()
+            ffn_cp[l, i] = cp
+
+    def ffn_recv(l, i):
+        b1 = (nz1, z1)[i]
+        ffn_cp[l, i].wait_recv()
+        for k in range(3):
+            GS[b1, z0, k] = GS[b1, z0, k] + RZ1[i, k]
+        if l > 0:
+            pl.semaphore_signal(cr_ffn.at[i], inc=1, device_id=pz0, device_id_type=MESH)
+        if i == 0:
+            if l < L - 1:
+                pl.semaphore_wait(cr_ffn.at[2], 1)
+            cp = remote(GS.at[nz1, z0], RZ2, fz_s.at[2], fz_r.at[2], pz1)
+            cp.start()
+            ffn_cp[l, 2] = cp
+
+    def ffn_last(l):
+        ffn_cp[l, 2].wait_recv()
+        for k in range(3):
+            GS[z1, z0, k] = GS[z1, z0, k] + RZ2[k]
+        if l > 0:
+            pl.semaphore_signal(cr_ffn.at[2], inc=1, device_id=pz1, device_id_type=MESH)
+        out_cols = pl.ds(pl.multiple_of(q * FQ, 128), FQ)
+
+        def rows_of(xx, yy):
+            return GS.at[z1, z0, :, pl.ds(pl.multiple_of((yy * 2 + xx) * R, 16), R), :]
+
+        cps = []
+        for j, (xx, yy, peer) in enumerate(((nx, y, px), (x, ny, py), (nx, ny, pxy))):
+            cp = remote(rows_of(xx, yy), offn.at[l, :, :, out_cols], fa_s.at[l, j], fa_r.at[l, j], peer)
+            cp.start()
+            cps.append(cp)
+        own = pltpu.make_async_copy(rows_of(x, y), offn.at[l, :, :, out_cols], fl.at[l])
+        own.start()
+        ffn_cp[l, 3] = (cps, own)
+
+    def ffn_sent(l):
+        for i in range(3):
+            ffn_cp[l, i].wait_send()
+        cps, own = ffn_cp[l, 3]
+        for cp in cps:
+            cp.wait_send()
+        own.wait()
+
+    def ffn_arrived(l):
+        for cp in ffn_cp[l, 3][0]:
+            cp.wait_recv()
+
+    def gn_step(step):
+        peer = (px, py, pz0, pz1)[step]
+        cp = remote(gn, gnr.at[step], gn_s.at[step], gn_r.at[step], peer)
+        cp.start()
+        cp.wait()
+        gn[...] = gn[...] + gnr[step]
+
+    def x_in(rows):
+        return x_ref[rows, :].astype(F32)
+
+    def x_now(rows):
+        return xcur[rows, :]
+
+    def cot_in(rows):
+        return cot_ref[rows, :].astype(F32)
+
+    ag_cp = {}
+    for l in range(L):
+        ag_cp[l] = forward(l, x_in if l == 0 else x_now)
+
+    dy_rows = cot_in
+    bwd_norm2(L - 1, dy_rows)
+    local = ag_local(L)
+    for l in reversed(range(L)):
+        k = 2 * L - 1 - l
+        bwd_hidden(l)
+        if l == L - 1:
+            ag_cp[k] = ag_send(k, local)
+        cps = bwd_ffn_sum(l)
+        if l < L - 1:
+            for kk in range(4):
+                att_recv(l + 1, kk, 0)
+        psum_wait(cps)
+        bwd_norm1(l)
+        bwd_attention(l)
+        cps = bwd_qkv_sum(l)
+        att_grad_prepare(l)
+        if l < L - 1:
+            ffn_recv(l + 1, 0)
+            for kk in range(4):
+                att_recv(l + 1, kk, 1)
+            ffn_recv(l + 1, 1)
+            for kk in range(4):
+                att_recv(l + 1, kk, 2)
+            ffn_last(l + 1)
+            for kk in range(4):
+                att_recv(l + 1, kk, 3)
+            for kk in range(4):
+                att_done(l + 1, kk)
+        for kk in range(4):
+            att_grad(l, kk)
+        psum_wait(cps)
+        for rows in row_chunks:
+            dx = acur[rows, :] + psum_rows(1, rows)
+            if l == 0:
+                igrad_ref[rows, :] = dx
+            else:
+                xcur[rows, :] = dx
+        if l > 0:
+            bwd_norm2(l - 1, x_now)
+            local = ag_local(k + 1)
+            ag_cp[k + 1] = ag_send(k + 1, local)
+        if l < L - 1:
+            ffn_sent(l + 1)
+        for kk in (l, k):
+            for cp in ag_cp[kk]:
+                cp.wait()
+        ffn_hidden(l)
+        for i in range(4):
+            ffn_block(l, i)
+
+    for step in range(4):
+        gn_step(step)
+    ffn_recv(0, 0)
+    for kk in range(4):
+        att_recv(0, kk, 0)
+    for kk in range(4):
+        att_recv(0, kk, 1)
+    ffn_recv(0, 1)
+    for kk in range(4):
+        att_recv(0, kk, 2)
+    ffn_last(0)
+    for kk in range(4):
+        att_recv(0, kk, 3)
+    for kk in range(4):
+        att_done(0, kk)
+    ffn_sent(0)
+    for l in range(L):
+        ffn_arrived(l)
+
+
+def fused(inputs, lengths, w_qkv, w_out, w_in, w_down, norm_gain, norm_bias, cotangent):
+    T, D = inputs.shape
+    L, _, _, E = w_qkv.shape
+    F = w_in.shape[-1]
+    W, NP, NC, FQ = T // 128, E // 128, D // 256, F // PLANE
+    R, RB = D // DP, D // (DP // PLANE)
+    vmem = pl.BlockSpec(memory_space=pltpu.VMEM)
+    smem = pl.BlockSpec(memory_space=pltpu.SMEM)
+    hbm = pl.BlockSpec(memory_space=pl.ANY)
+    V = pltpu.VMEM
+    DMA = pltpu.SemaphoreType.DMA
+    REG = pltpu.SemaphoreType.REGULAR
+    scratch = [
+        V((L, 3, D, E), BF16), V((L, E, D), BF16), V((L, 2, D, F), BF16), V((L, F, D), BF16),
+        V((L, T, D), BF16), V((L, 3, T, E), BF16), V((L, W, NP, 128, 256), BF16), V((L, T, E), BF16),
+        V((L, T, D), BF16), V((L, T, D), BF16), V((L, T, 1), F32), V((L, T, 1), F32),
+        V((T, D), F32), V((T, D), F32), V((T, D), BF16),
+        V((2, NC, T, 256), F32), V((2, NC, T, 256), F32),
+        V((T, F), BF16), V((L, 2, T, F), BF16), V((T, E), BF16), V((3, T, E), BF16),
+        V((D, T), BF16), V((D, T), BF16),
+        V((D, PLANE * T), BF16), V((D, PLANE * T), BF16), V((PLANE * T, 3 * FQ), BF16),
+        V((2, 2, T, D), F32),
+        V((2, 2, 3, RB, FQ), F32), V((2, 3, RB, FQ), F32), V((3, RB, FQ), F32),
+        V((4, 2, 2, 2, 2, R, E), F32), V((4, 2, 2, 2, R, E), F32), V((4, 2, 2, R, E), F32),
+        V((4, 2, R, E), F32), V((4, R, E), F32),
+        V((4, 4 * L, D), F32),
+        DMA((L, 4)), DMA((2, NC)), DMA((2, NC)), DMA((2 * L,)), DMA((2 * L, 3)), DMA((2 * L, 3)), DMA((2, 2)),
+        DMA((3,)), DMA((3,)), DMA((L, 3)), DMA((L, 3)), DMA((L,)), DMA((4, 4)), DMA((4, 4)), DMA((4,)),
+        DMA((4,)), DMA((4,)), REG((4, 4)), REG((3,)),
+    ]
+    outs = pl.pallas_call(
+        functools.partial(kernel, T, D, E, F, L),
+        out_shape=(
+            jax.ShapeDtypeStruct((T, D), BF16),
+            jax.ShapeDtypeStruct((T, D), F32),
+            jax.ShapeDtypeStruct((L, 4, R, E), F32),
+            jax.ShapeDtypeStruct((L, 3, R, F), F32),
+            jax.ShapeDtypeStruct((4 * L, D), F32),
+            jax.ShapeDtypeStruct((2 * L, PLANE, T, D), F32),
+        ),
+        in_specs=[smem, vmem, vmem, vmem, vmem, hbm, hbm, hbm, hbm],
+        out_specs=(vmem, vmem, hbm, hbm, vmem, hbm),
+        scratch_shapes=scratch,
+        compiler_params=pltpu.CompilerParams(collective_id=0, has_side_effects=True, vmem_limit_bytes=63 * 2**20),
+        name="encoder",
+    )(lengths, inputs, cotangent, norm_gain, norm_bias, w_qkv, w_out, w_in, w_down)
+    encoded, input_grad, oatt, offn, gn, _ = outs
+    mine = lax.dynamic_slice_in_dim(gn.reshape(2, L, 2, D), lax.axis_index("dp") * R, R, axis=3)
+    return (
+        encoded,
+        input_grad,
+        oatt[:, :3],
+        jnp.swapaxes(oatt[:, 3], 1, 2),
+        offn[:, :2],
+        jnp.swapaxes(offn[:, 2], 1, 2),
+        mine[0],
+        mine[1],
+    )
 
 
 def normalize(values, gain_vec, shift_vec):
@@ -216,7 +808,7 @@
 
 def solution(mesh):
     return jax.shard_map(
-        body,
+        fused if mesh.shape["dp"] == DP and mesh.shape["tensor"] == 2 else body,
         mesh=mesh,
         in_specs=(
             P("dp", None),

time: 1580 us -> 337 us (0.21)
  waiting for transfers between devices: 1310 us -> 0 us
  Pallas kernels: 0 us -> 326 us
  local copies, waits for them, and re-layouts: 109 us -> 10.1 us
  matrix products: 76.8 us -> 0 us
  other arithmetic: 50.4 us -> 0 us
  between operations: 16.7 us -> 0.68 us
    unnamed x16 -> x0, waiting for transfers between devices: 1160 us -> none
    pallas_call x0 -> x1, Pallas kernels: none -> 326 us  [fused(): pl.pallas_call(functools.partial(kernel, T, D, E, F, L), out_shape=(jax.S...]
    psum x8 -> x0, waiting for transfers between devices: 155 us -> none  [the longest x2 41.6 us: layer_forward(): lax.psum(jnp.dot(mixed_heads, out_weight, preferred_element_type=jnp.floa...]
    dot_general x36 -> x0, matrix products: 76.8 us -> none  [the longest x2 9.87 us: layer_forward(): jnp.dot(gated_low, down_weight, preferred_element_type=jnp.float32)]
    another operation x16 -> x0, local copies, waits for them, and re-layouts: 66.8 us -> none  [the longest x4 62.5 us: body(): jnp.stack([pieces[index][member] for index in range(layers)])]
    another operation x14 -> x0, other arithmetic: 30.1 us -> none  [the longest x10 21.7 us: body(): jnp.stack([pieces[index][member] for index in range(layers)])]
    unnamed x243 -> x8, local copies, waits for them, and re-layouts: 30.6 us -> 1.64 us
    reduce_sum x18 -> x0, other arithmetic: 16.8 us -> none  [the longest x8 8.18 us: normalize(): center = values - jnp.mean(values, -1, keepdims=True)]
  transfers between devices with their start and end apart: 12 -> 0, of which waited for: 12 -> 0; matrix products, arithmetic and copies ran while one was open for 8% -> 0% of each run, Pallas kernels for 0% -> 0%
where the time goes in v1:
time: 337 us
  Pallas kernels  326 us (97%)
  local copies, waits for them, and re-layouts  10.1 us (3%)
    pallas_call x1, Pallas kernels, fused(): pl.pallas_call(functools.partial(kernel, T, D, E, F, L), out_shape=(jax.S...  326 us

profile of v1, /device:TPU:0, one launch (start us, length us, event | category | flops | bytes accessed | tf_op | source)
XLA Modules:
  0.0 337.0 jit_solution(16793117022561767898)
XLA Ops:
  0.6 326.2 %encoder.1 = (bf16[256,768]{1,0:T(8,128)(2,1)}, f32[256,768]{1,0:T(8,128)}, f32[2,4,48,384]{3,2,1,0:T(8,128)}, f32[2,3,48,1536]{3,2,1,0:T(8,128)}, f32[8,768]{1,0:T(8,128)}, /*index=5*/f32[4,4,256,768]{3,2,1,0:T(8,128)}) custom-call(s32[2]{0:T(128)} %len_ref.1, bf16[256,768]{1,0:T(8,128)(2,1)} %x_ref.1, bf16[256,768]{1,0:T(8,128)(2,1)} %cot_ref.1, ...), custom_call_target="tpu_custom_call" | custom-call | tf_op jit(solution)/shard_map/encoder/pallas_call | solution.py:576
  326.8 0.0 copy-start.2
  326.9 0.0 copy-start.1
  326.9 0.0 copy-start
  326.9 1.9 slice.18
  328.8 1.6 slice_bitcast_fusion.1
  330.4 2.4 slice.20
  332.7 1.9 slice_bitcast_fusion
  334.6 0.0 copy-done.2
  334.7 0.7 dynamic-slice_bitcast_fusion
  335.3 0.0 copy-done.1
  335.3 0.7 copy.19
  336.1 0.0 copy-done
  336.1 0.9 copy.20
  (1 shorter events, 0.0 us)
Async XLA Ops:
  326.8 7.8 %copy-start.2 = (f32[8,768]{1,0:T(8,128)S(1)}, f32[8,768]{1,0:T(8,128)}, u32[]{:S(2)}) copy-start(f32[8,768]{1,0:T(8,128)} %get-tuple-element.17) | copy-start | bytes 73732
  326.9 8.5 %copy-start.1 = (bf16[256,768]{1,0:T(8,128)(2,1)S(1)}, bf16[256,768]{1,0:T(8,128)(2,1)}, u32[]{:S(2)}) copy-start(bf16[256,768]{1,0:T(8,128)(2,1)} %get-tuple-element.28) | copy-start | bytes 1179652
  326.9 9.2 %copy-start = (f32[256,768]{1,0:T(8,128)S(1)}, f32[256,768]{1,0:T(8,128)}, u32[]{:S(2)}) copy-start(f32[256,768]{1,0:T(8,128)} %get-tuple-element.29) | copy-start | bytes 2359300

commit v2 on v0

--- a/solution.py
+++ b/solution.py
@@ -1,14 +1,826 @@
+import functools
+
 import jax
 import jax.numpy as jnp
 from jax import lax
+from jax.experimental import pallas as pl
+from jax.experimental.pallas import tpu as pltpu
 from jax.sharding import PartitionSpec as P
 
 HEADS = 12
 HEAD_DIM = 64
-
-
 EPS = 1e-05
 MASKED = -1000000000.0
+MESH = pl.DeviceIdType.MESH
+F32 = jnp.float32
+BF16 = jnp.bfloat16
+GROUP = 4
+DP = 16
+AXES = ("z1", "z0", "y", "x")
+SHARE = (("z1", "y"), ("z0", "x"))
+FFN = ((("x", "z0"), ("z0", "x")), (("y", "z1"), ("z1", "y")))
+PAIR = ("z0", "y")
+ATT = ((("y", "x", "z1"), ("y", "x", "z1")), (("z0", "z1", "x"), ("x", "z0", "z1")))
+
+
+def dot(a, b):
+    return lax.dot_general(a, b, (((1,), (0,)), ((), ())), preferred_element_type=F32)
+
+
+def dot_t(a, b):
+    return lax.dot_general(a, b, (((1,), (1,)), ((), ())), preferred_element_type=F32)
+
+
+def dot_tt(a, b):
+    return lax.dot_general(a, b, (((0,), (0,)), ((), ())), preferred_element_type=F32)
+
+
+def gelu_parts(g):
+    bell = jnp.exp(-0.5 * g * g)
+    d = 1.0 + (0.3275911 * 0.7071067811865476) * jnp.abs(g)
+    t = pl.reciprocal(d, approx=True)
+    t = t * (2.0 - d * t)
+    poly = t * (0.127414796 + t * (-0.142248368 + t * (0.7107068705 + t * (-0.7265760135 + t * 0.5307027145))))
+    tail = poly * bell
+    phi = jnp.where(g >= 0, 1.0 - tail, tail)
+    return g * phi, phi + g * (bell * 0.3989422804014327)
+
+
+def kernel(
+    T, D, E, F, L,
+    len_ref, x_hbm, cot_hbm, gain_ref, bias_ref, wq_hbm, wo_hbm, wi_hbm, wd_hbm,
+    enc_ref, igrad_ref, oatt, offn, gn, ag, az,
+    wq, wo, wi, wd, xb, qkv, pb, om, hhat, zhat, hr, zr, xcur, acur, ab, psend, precv, eb, AB,
+    LT, LA, abT, dfbT, wab, wdfb, lens, GF, RF1, RF2, GA, RA1, RA2, RA3, gnr,
+    wsem, insem, ps_s, ps_r, agl, aga_s, aga_r, agb_s, agb_r, agf_s, agf_r, agc_s, agc_r,
+    ln_s, ln_r, igl, azl, azz_s, azz_r, azc_s, azc_r, stsem, fz_s, fz_r, fa_s, fa_r, fl, at_s, at_r, ato_s, ato_r, atl, gn_s, gn_r,
+):
+    dp = lax.axis_index("dp")
+    c = lax.axis_index("tensor")
+    weight = {"x": 1, "y": 2, "z0": 4, "z1": 8}
+    me = {a: lax.rem(lax.div(dp, w), 2) for a, w in weight.items()}
+    other = {a: 1 - me[a] for a in AXES}
+
+    def peer(*axes):
+        return (dp + sum(weight[a] * (1 - 2 * me[a]) for a in axes), c)
+
+    sib = (dp, 1 - c)
+    W = T // 128
+    NP = E // 128
+    FQ = F // GROUP
+    NC = D // 256
+    R = D // DP
+    HT = T // 2
+    QL = E
+
+    barrier = pltpu.get_barrier_semaphore()
+    friends = [sib] + [peer(a) for a in AXES] + [peer(*p) for p in sorted(set(SHARE))]
+    for friend in friends:
+        pl.semaphore_signal(barrier, inc=1, device_id=friend, device_id_type=MESH)
+    pl.semaphore_wait(barrier, len(friends))
+
+    def remote(src, dst, ss, rs, to):
+        cp = pltpu.make_async_remote_copy(
+            src_ref=src, dst_ref=dst, send_sem=ss, recv_sem=rs, device_id=to, device_id_type=MESH
+        )
+        cp.start()
+        return cp
+
+    def here(src, dst, sem):
+        cp = pltpu.make_async_copy(src, dst, sem)
+        cp.start()
+        return cp
+
+    wcopies = {}
+    x_cp = here(x_hbm, ab, insem.at[0])
+    for l in range(L):
+        for i, (src, dst) in enumerate(((wq_hbm, wq), (wo_hbm, wo), (wi_hbm, wi), (wd_hbm, wd))):
+            wcopies[l, i] = here(src.at[l], dst.at[l], wsem.at[l, i])
+
+    RC = 64
+    row_chunks = [pl.ds(r, RC) for r in range(0, T, RC)]
+
+    def psum_send(slot, part):
+        cps = []
+        for n in range(NC):
+            cols = pl.ds(n * 256, 256)
+            psend[slot, :, cols] = part(n)
+            cps.append(remote(psend.at[slot, :, cols], precv.at[slot, :, cols], ps_s.at[slot, n], ps_r.at[slot, n], sib))
+        return cps
+
+    def psum_wait(cps):
+        for cp in cps:
+            cp.wait()
+
+    def psum_rows(slot, rows):
+        return psend[slot, rows, :] + precv[slot, rows, :]
+
+    def norm_rows(v):
+        center = v - jnp.mean(v, -1, keepdims=True)
+        r = lax.rsqrt(jnp.mean(center * center, -1, keepdims=True) + EPS)
+        return center * r, r
+
+    def ln_bwd_rows(dy, hat, r, gain):
+        t = dy * gain
+        m1 = jnp.mean(t, -1, keepdims=True)
+        m2 = jnp.mean(t * hat, -1, keepdims=True)
+        return r * (t - m1 - hat * m2)
+
+    half = pl.ds(pl.multiple_of(c * HT, 128), HT)
+
+    class Group:
+        def __init__(self, k):
+            A, B = SHARE[min(k, 2 * L - 1 - k)]
+            self.k, self.A, self.B = k, A, B
+            self.slots = {"own": (me[A], me[B]), "A": (other[A], me[B]), "B": (me[A], other[B]), "AB": (other[A], other[B])}
+
+        def slot(self, name):
+            i, j = self.slots[name]
+            return ag.at[self.k, i, j]
+
+        def keep(self, src):
+            self.own = here(src, self.slot("own"), agl.at[self.k])
+
+        def send(self, src=None):
+            k = self.k
+            mine = self.slot("own").at[half]
+            if src is None:
+                self.own.wait()
+                src = mine
+            else:
+                src = src.at[half]
+            self.ac = remote(src, mine, aga_s.at[k], aga_r.at[k], peer(self.A))
+            self.bc = remote(src, mine, agb_s.at[k], agb_r.at[k], peer(self.B))
+
+        def forward(self):
+            k = self.k
+            self.ac.wait_recv()
+            ref = self.slot("A").at[half]
+            self.fc = remote(ref, ref, agf_s.at[k], agf_r.at[k], peer(self.B))
+
+        def share(self):
+            k = self.k
+            self.bc.wait_recv()
+            self.fc.wait_recv()
+            self.cc = []
+            for j, name in enumerate(("A", "B", "AB")):
+                ref = self.slot(name).at[half]
+                self.cc.append(remote(ref, ref, agc_s.at[k, j], agc_r.at[k, j], sib))
+
+        def sent(self):
+            self.ac.wait_send()
+            self.bc.wait_send()
+
+        def ready(self):
+            for cp in self.cc:
+                cp.wait()
+            self.fc.wait_send()
+
+    class Pair:
+        def __init__(self, k):
+            self.k, self.axis = k, PAIR[min(k, 2 * L - 1 - k)]
+
+        def keep(self, src):
+            self.own = here(src, az.at[self.k, me[self.axis]], azl.at[self.k])
+
+        def send(self):
+            k = self.k
+            self.own.wait()
+            mine = az.at[k, me[self.axis], half]
+            self.zc = remote(mine, mine, azz_s.at[k], azz_r.at[k], peer(self.axis))
+
+        def share(self):
+            k = self.k
+            self.zc.wait()
+            ref = az.at[k, other[self.axis], half]
+            self.cc = remote(ref, ref, azc_s.at[k], azc_r.at[k], sib)
+
+        def ready(self):
+            self.cc.wait()
+
+    for w in range(W):
+        lens[0, pl.ds(w, 1), :] = jnp.full((1, 128), len_ref[w], jnp.int32).astype(F32)
+    len_cp = [remote(lens.at[0], lens.at[1 + l], ln_s.at[l], ln_r.at[l], peer(PAIR[l])) for l in range(L)]
+
+    def dfb_index(l):
+        return 2 * L - 1 - l
+
+    groups = [Group(k) for k in range(2 * L)]
+    pairs = [Pair(k) for k in range(2 * L)]
+
+    lane = lax.broadcasted_iota(jnp.int32, (128, 128), 1)
+    first = lane < HEAD_DIM
+    dist = jnp.abs(lax.broadcasted_iota(jnp.int32, (128, 128), 0) - lane).astype(F32)
+    scale = HEAD_DIM ** -0.5
+
+    def halves(v):
+        zero = jnp.zeros_like(v)
+        return jnp.concatenate([jnp.where(first, v, zero), jnp.where(first, zero, v)], axis=0)
+
+    def pick(table, index):
+        s = jnp.float32(table[0])
+        for i in range(1, len(table)):
+            s = jnp.where(index == i, jnp.float32(table[i]), s)
+        return s
+
+    heads_local = E // HEAD_DIM
+    slopes = [2.0 ** (-8.0 * (h + 1.0) / HEADS) for h in range(HEADS)]
+
+    def slope(h):
+        return pick(slopes[h::heads_local], c)
+
+    def slope_outer(i, side):
+        table = []
+        for cc in range(HEADS // heads_local):
+            table += [slopes[cc * heads_local + i], slopes[cc * heads_local + 2 * (NP - 1) + i]]
+        return pick(table, 2 * c + side)
+
+    def attend(qq, kk, vv, live, slope_pair):
+        s = dot_t(qq, kk)
+        both = []
+        for i in range(2):
+            si = s[:, i * 128:(i + 1) * 128] * scale - slope_pair[i] * dist
+            si = jnp.where(live, si, MASKED)
+            ei = jnp.exp(si - jnp.max(si, -1, keepdims=True))
+            both.append(ei * (1.0 / jnp.sum(ei, -1, keepdims=True)))
+        prob = jnp.concatenate(both, axis=1).astype(BF16)
+        return prob, dot(prob, vv).astype(BF16)
+
+    def attend_bwd(qq, kk, vv, prob, do):
+        dprob = dot_t(do, vv)
+        p32 = prob.astype(F32)
+        both = []
+        for i in range(2):
+            pi, di = p32[:, i * 128:(i + 1) * 128], dprob[:, i * 128:(i + 1) * 128]
+            both.append(pi * (di - jnp.sum(pi * di, -1, keepdims=True)))
+        ds = jnp.concatenate(both, axis=1).astype(BF16)
+        dv2 = dot_tt(prob, do)
+        dk2 = dot_tt(ds, qq)
+        dq = (dot(ds, kk) * scale).astype(BF16)
+        dk = (jnp.where(first, dk2[:128], dk2[128:]) * scale).astype(BF16)
+        dv = jnp.where(first, dv2[:128], dv2[128:]).astype(BF16)
+        return dq, dk, dv
+
+    def nothing():
+        pass
+
+    def fwd_attention(l, mid=nothing):
+        pairs[l].keep(xcur)
+        for rows in row_chunks:
+            xb[l, rows, :] = xcur[rows, :].astype(BF16)
+        wcopies[l, 0].wait()
+        for k in range(3):
+            qkv[l, k] = dot(xb[l], wq[l, k]).astype(BF16)
+        pairs[l].send()
+        mid()
+
+        def window(w, _):
+            rows = pl.ds(pl.multiple_of(w * 128, 128), 128)
+            live = lane < len_ref[w]
+            for p in range(NP):
+                cols = pl.ds(p * 128, 128)
+                kk, vv = halves(qkv[l, 1, rows, cols]), halves(qkv[l, 2, rows, cols])
+                prob, out = attend(qkv[l, 0, rows, cols], kk, vv, live, (slope(2 * p), slope(2 * p + 1)))
+                pb[l, w, p] = prob
+                om[l, rows, cols] = out
+            return 0
+
+        lax.fori_loop(0, W, window, 0)
+        wcopies[l, 1].wait()
+        return psum_send(0, lambda n: dot(om[l], wo[l, :, pl.ds(n * 256, 256)]))
+
+    def fwd_norm1(l, cps):
+        psum_wait(cps)
+        gain, bias = gain_ref[l, 0:1, :], bias_ref[l, 0:1, :]
+        for rows in row_chunks:
+            hat, r = norm_rows(xcur[rows, :] + psum_rows(0, rows))
+            hhat[l, rows, :] = hat.astype(BF16)
+            hr[l, rows, :] = r
+            a = hat * gain + bias
+            acur[rows, :] = a
+            ab[rows, :] = a.astype(BF16)
+        groups[l].keep(acur)
+
+    def fwd_ffn(l, mid=nothing):
+        wcopies[l, 2].wait()
+
+        def hidden(j, _):
+            cols = pl.ds(pl.multiple_of(j * 256, 256), 256)
+            g = dot(ab[...], wi[l, 0, :, cols])
+            u = dot(ab[...], wi[l, 1, :, cols])
+            act, slope_g = gelu_parts(g)
+            eb[:, cols] = (act * u).astype(BF16)
+            AB[l, 0, :, cols] = act.astype(BF16)
+            AB[l, 1, :, cols] = (slope_g * u).astype(BF16)
+            return 0
+
+        lax.fori_loop(0, 2, hidden, 0)
+        groups[l].send()
+        lax.fori_loop(2, F // 256, hidden, 0)
+        mid()
+        wcopies[l, 3].wait()
+        return psum_send(1, lambda n: dot(eb[...], wd[l, :, pl.ds(n * 256, 256)]))
+
+    def fwd_norm2(l, cps):
+        psum_wait(cps)
+        gain, bias = gain_ref[l, 1:2, :], bias_ref[l, 1:2, :]
+        for rows in row_chunks:
+            hat, r = norm_rows(acur[rows, :] + psum_rows(1, rows))
+            zhat[l, rows, :] = hat.astype(BF16)
+            zr[l, rows, :] = r
+            out = hat * gain + bias
+            if l == L - 1:
+                enc_ref[rows, :] = out.astype(BF16)
+            else:
+                xcur[rows, :] = out
+
+    def bwd_norm2(l, dy_rows):
+        gain = gain_ref[l, 1:2, :]
+        dg = jnp.zeros((1, D), F32)
+        db = jnp.zeros((1, D), F32)
+        for rows in row_chunks:
+            dy = dy_rows(rows)
+            hat = zhat[l, rows, :].astype(F32)
+            dz = ln_bwd_rows(dy, hat, zr[l, rows, :], gain)
+            acur[rows, :] = dz
+            ab[rows, :] = dz.astype(BF16)
+            dg = dg + jnp.sum(dy * hat, 0, keepdims=True)
+            db = db + jnp.sum(dy, 0, keepdims=True)
+        gn[pl.ds(2 * l + 1, 1), :] = dg
+        gn[pl.ds(2 * L + 2 * l + 1, 1), :] = db
+        groups[dfb_index(l)].send(acur)
+        groups[dfb_index(l)].keep(acur)
+
+    def bwd_ffn(l, mid=nothing):
+        def hidden(j, _):
+            cols = pl.ds(pl.multiple_of(j * 256, 256), 256)
+            de = dot_t(ab[...], wd[l, cols, :])
+            dg = de * AB[l, 1, :, cols].astype(F32)
+            du = de * AB[l, 0, :, cols].astype(F32)
+            AB[l, 0, :, cols] = dg.astype(BF16)
+            AB[l, 1, :, cols] = du.astype(BF16)
+            return 0
+
+        lax.fori_loop(0, F // 256, hidden, 0)
+        mid()
+        return psum_send(
+            0,
+            lambda n: dot_t(AB[l, 0], wi[l, 0, pl.ds(n * 256, 256), :]) + dot_t(AB[l, 1], wi[l, 1, pl.ds(n * 256, 256), :]),
+        )
+
+    def bwd_norm1(l, cps):
+        psum_wait(cps)
+        gain = gain_ref[l, 0:1, :]
+        dg = jnp.zeros((1, D), F32)
+        db = jnp.zeros((1, D), F32)
+        for rows in row_chunks:
+            da = acur[rows, :] + psum_rows(0, rows)
+            hat = hhat[l, rows, :].astype(F32)
+            dh = ln_bwd_rows(da, hat, hr[l, rows, :], gain)
+            xcur[rows, :] = dh
+            ab[rows, :] = dh.astype(BF16)
+            dg = dg + jnp.sum(da * hat, 0, keepdims=True)
+            db = db + jnp.sum(da, 0, keepdims=True)
+        gn[pl.ds(2 * l, 1), :] = dg
+        gn[pl.ds(2 * L + 2 * l, 1), :] = db
+        pairs[dfb_index(l)].keep(xcur)
+
+    def dqkv(k):
+        return pl.ds(k * QL, QL)
+
+    def bwd_attention(l, mid=nothing, late=nothing):
+        eb[:, dqkv(3)] = dot_t(ab[...], wo[l]).astype(BF16)
+        pairs[dfb_index(l)].send()
+        mid()
+
+        def window(w, _):
+            rows = pl.ds(pl.multiple_of(w * 128, 128), 128)
+            for p in range(NP):
+                cols = pl.ds(p * 128, 128)
+                kk, vv = halves(qkv[l, 1, rows, cols]), halves(qkv[l, 2, rows, cols])
+                grads = attend_bwd(qkv[l, 0, rows, cols], kk, vv, pb[l, w, p], eb[rows, pl.ds(3 * QL + p * 128, 128)])
+                for k in range(3):
+                    eb[rows, pl.ds(k * QL + p * 128, 128)] = grads[k]
+            return 0
+
+        lax.fori_loop(0, W, window, 0)
+        late()
+        return psum_send(
+            1,
+            lambda n: sum(dot_t(eb[:, dqkv(k)], wq[l, k, pl.ds(n * 256, 256), :]) for k in range(3)),
+        )
+
+    def bwd_input(l, cps):
+        psum_wait(cps)
+        for rows in row_chunks:
+            dx = xcur[rows, :] + psum_rows(1, rows)
+            xcur[rows, :] = dx
+
+    middle = 128
+
+    def side_of(l):
+        side = me[PAIR[l]]
+        return side, pl.multiple_of(side * (E - 128), 128)
+
+    def att_own(l):
+        side, outer = side_of(l)
+        own = pl.ds(0, T)
+        LT[0, :, own] = xb[l].T
+        LT[1, :, own] = ab[...].T
+        for k in range(3):
+            LA[own, pl.ds(k * 128, 128)] = eb[:, pl.ds(pl.multiple_of(k * QL + outer, 128), 128)]
+        LA[own, pl.ds(3 * 128, 128)] = om[l, :, pl.ds(outer, 128)]
+        low = side == 0
+        LA[own, pl.ds(4 * 128, 128)] = jnp.where(low, eb[:, pl.ds(middle, 128)], eb[:, pl.ds(2 * QL + middle, 128)])
+        LA[own, pl.ds(5 * 128, 128)] = jnp.where(low, eb[:, pl.ds(QL + middle, 128)], om[l, :, pl.ds(middle, 128)])
+
+    def att_partner(l):
+        k2 = dfb_index(l)
+        side, outer = side_of(l)
+        partner = other[PAIR[l]]
+        pairs[l].ready()
+        pairs[k2].ready()
+        len_cp[l].wait()
+        c0 = here(az.at[l, partner], psend.at[0], stsem.at[0])
+        c1 = here(az.at[k2, partner], psend.at[1], stsem.at[1])
+        c0.wait()
+        c1.wait()
+        wab[...] = psend[0].astype(BF16)
+        wdfb[...] = psend[1].astype(BF16)
+        far = pl.ds(T, T)
+        LT[0, :, far] = wab[...].T
+        LT[1, :, far] = wdfb[...].T
+        for k in range(3):
+            wcols = jnp.concatenate([wq[l, k, :, pl.ds(outer, 128)], wq[l, k, :, pl.ds(middle, 128)]], axis=1)
+            AB[0, 0, :, pl.ds(k * 256, 256)] = dot(wab[...], wcols).astype(BF16)
+        wrows = jnp.concatenate([wo[l, pl.ds(outer, 128), :], wo[l, pl.ds(middle, 128), :]], axis=0)
+        AB[0, 0, :, pl.ds(3 * 256, 256)] = dot_t(wdfb[...], wrows).astype(BF16)
+        low = side == 0
+
+        def window(w, _):
+            rows = pl.ds(pl.multiple_of(w * 128, 128), 128)
+            dest = pl.ds(pl.multiple_of(T + w * 128, 128), 128)
+            live = lane.astype(F32) < lens[1 + l, pl.ds(w, 1), :]
+            for p in range(2):
+                qq, kk, vv, do = (AB[0, 0, rows, pl.ds(k * 256 + p * 128, 128)] for k in range(4))
+                kk, vv = halves(kk), halves(vv)
+                pair = (slope_outer(0, side), slope_outer(1, side)) if p == 0 else (slope(2), slope(3))
+                prob, out = attend(qq, kk, vv, live, pair)
+                dq, dk, dv = attend_bwd(qq, kk, vv, prob, do)
+                if p == 0:
+                    for k, v in enumerate((dq, dk, dv, out)):
+                        LA[dest, pl.ds(k * 128, 128)] = v
+                else:
+                    LA[dest, pl.ds(4 * 128, 128)] = jnp.where(low, dq, dv)
+                    LA[dest, pl.ds(5 * 128, 128)] = jnp.where(low, dk, out)
+            return 0
+
+        lax.fori_loop(0, W, window, 0)
+
+    def place(at):
+        return tuple(at[a] for a in AXES)
+
+    def att_views(l, ch):
+        at = {a: slice(None) for a in AXES}
+        views = []
+        for axis, land in zip(ATT[l][ch], (RA1, RA2, RA3)):
+            send = GA.at[(l, ch) + place({**at, axis: other[axis]})]
+            at[axis] = me[axis]
+            views.append((send, GA.at[(l, ch) + place(at)], land.at[l, ch], axis))
+        return views
+
+    att_cp = {}
+
+    def att_send(l, ch, step):
+        send, _, land, axis = att_views(l, ch)[step]
+        att_cp[l, ch, step] = remote(send, land, at_s.at[l, ch, step], at_r.at[l, ch, step], peer(axis))
+
+    def att_grad(l, ch):
+        for b in range(3):
+            cols = pl.ds((3 * ch + b) * 128, 128)
+            left = LT.at[0] if 3 * ch + b in (0, 1, 2, 4) else LT.at[1] if 3 * ch + b == 3 else LT.at[me[PAIR[l]]]
+            GA[l, ch, :, :, :, :, b] = dot(left[...], LA[:, cols]).reshape(2, 2, 2, 2, R, 128)
+        att_send(l, ch, 0)
+
+    def att_recv(l, ch, step):
+        _, stay, land, _ = att_views(l, ch)[step]
+        att_cp[l, ch, step].wait_recv()
+        stay[...] = stay[...] + land[...]
+        if step < 2:
+            att_send(l, ch, step + 1)
+            return
+        axis = PAIR[l]
+        side, outer = side_of(l)
+        outer_cols = pl.ds(outer, 128)
+        if ch == 0:
+            moves = ((pl.ds(0, 3), oatt.at[l, pl.ds(0, 3), :, outer_cols]),)
+        else:
+            mid = pl.ds(middle, 128)
+            moves = (
+                (0, oatt.at[l, 3, :, outer_cols]),
+                (1, oatt.at[l, 2 * side, :, mid]),
+                (2, oatt.at[l, 1 + 2 * side, :, mid]),
+            )
+        for i, (b, dst) in enumerate(moves):
+            n = ch + i
+            far = GA.at[(l, ch) + place({**me, axis: other[axis]}) + (b,)]
+            att_cp[l, "out", n] = remote(far, dst, ato_s.at[l, n], ato_r.at[l, n], peer(axis))
+            att_cp[l, "own", n] = here(GA.at[(l, ch) + place(me) + (b,)], dst, atl.at[l, n])
+
+    def att_done(l):
+        for ch in range(2):
+            for step in range(3):
+                att_cp[l, ch, step].wait_send()
+        for n in range(4):
+            att_cp[l, "out", n].wait()
+            att_cp[l, "own", n].wait()
+
+    def qcols_of(l):
+        A, B = SHARE[l]
+        return pl.ds(pl.multiple_of((2 * me[A] + me[B]) * FQ, 128), FQ)
+
+    def ffn_hidden(l):
+        k2 = dfb_index(l)
+        qcols = qcols_of(l)
+
+        def load(s):
+            zz, xx = lax.div(s, 2), lax.rem(s, 2)
+            return (
+                pltpu.make_async_copy(ag.at[l, zz, xx], psend.at[0], stsem.at[0]),
+                pltpu.make_async_copy(ag.at[k2, zz, xx], psend.at[1], stsem.at[1]),
+            )
+
+        for cp in load(0):
+            cp.start()
+
+        def chunk(s, _):
+            zz, xx = lax.div(s, 2), lax.rem(s, 2)
+            for cp in load(s):
+                cp.wait()
+            wab[...] = psend[0].astype(BF16)
+            wdfb[...] = psend[1].astype(BF16)
+
+            @pl.when(s < GROUP - 1)
+            def _():
+                for cp in load(s + 1):
+                    cp.start()
+
+            toks = pl.ds(pl.multiple_of(s * T, T), T)
+            abT[:, toks] = wab[...].T
+            dfbT[:, toks] = wdfb[...].T
+            g = dot(wab[...], wi[l, 0, :, qcols])
+            u = dot(wab[...], wi[l, 1, :, qcols])
+            de = dot_t(wdfb[...], wd[l, qcols, :])
+            act, slope_g = gelu_parts(g)
+            AB[zz, xx, :, pl.ds(0, FQ)] = (de * u * slope_g).astype(BF16)
+            AB[zz, xx, :, pl.ds(FQ, FQ)] = (de * act).astype(BF16)
+            AB[zz, xx, :, pl.ds(2 * FQ, FQ)] = (act * u).astype(BF16)
+            return 0
+
+        lax.fori_loop(0, GROUP, chunk, 0)
+
+    ffn_cp = {}
+    kinds = (pl.ds(0, 2), pl.ds(2, 1))
+
+    def sum_axes(l):
+        return [a for a in AXES if a not in SHARE[l]]
+
+    def ffn_block(l, i):
+        (A, B), (r0, r1) = SHARE[l], sum_axes(l)
+        to0, to1 = i in (0, 1), i in (0, 2)
+        at0, at1 = other[r0] if to0 else me[r0], other[r1] if to1 else me[r1]
+        base = at0 * weight[r0] + at1 * weight[r1]
+        places = [base + i * weight[A] + j * weight[B] for i in range(2) for j in range(2)]
+        for k in range(3):
+            left = abT if k < 2 else dfbT
+            rows = jnp.concatenate([left[pl.ds(pl.multiple_of(p * R, 16), R), :] for p in places], axis=0)
+            right = jnp.concatenate([AB[i, j, :, pl.ds(k * FQ, FQ)] for i in range(2) for j in range(2)], axis=0)
+            GF[l, at0, at1, k] = dot(rows, right)
+        for ch in range(2):
+            if i == 0:
+                ffn_send(l, ch, 0)
+            elif i == (1 if FFN[l][ch][0] == r0 else 2):
+                ffn_send(l, ch, 1)
+
+    def ffn_views(l, ch):
+        k = kinds[ch]
+        first, second = FFN[l][ch]
+
+        def block(at):
+            return GF.at[(l,) + tuple(at[a] for a in sum_axes(l)) + (k,)]
+
+        both, one, two = {first: other[first], second: other[second]}, {**me, first: other[first]}, {**me, second: other[second]}
+        return (
+            (block(both), block(two), RF1.at[l, 0, k], first),
+            (block(one), block(me), RF1.at[l, 1, k], first),
+            (block(two), block(me), RF2.at[l, k], second),
+        )
+
+    def ffn_send(l, ch, i):
+        src, _, land, axis = ffn_views(l, ch)[i]
+        ffn_cp[l, ch, i] = remote(src, land, fz_s.at[l, ch, i], fz_r.at[l, ch, i], peer(axis))
+
+    def ffn_recv(l, ch, i):
+        _, stay, land, _ = ffn_views(l, ch)[i]
+        ffn_cp[l, ch, i].wait_recv()
+        stay[...] = stay[...] + land[...]
+        if i == 0:
+            ffn_send(l, ch, 2)
+        if i < 2:
+            return
+        dst = offn.at[l, kinds[ch], :, qcols_of(l)]
+        A, B = SHARE[l]
+        final = [me[a] for a in sum_axes(l)]
+
+        def rows_of(i, j):
+            return GF.at[l, final[0], final[1], kinds[ch], pl.ds(pl.multiple_of((2 * i + j) * R, 16), R), :]
+
+        ffn_cp[l, ch, "out"] = [
+            remote(rows_of(i, j), dst, fa_s.at[l, ch, n], fa_r.at[l, ch, n], to)
+            for n, (i, j, to) in enumerate(
+                ((me[A], other[B], peer(B)), (other[A], me[B], peer(A)), (other[A], other[B], peer(A, B)))
+            )
+        ]
+        ffn_cp[l, ch, "own"] = here(rows_of(me[A], me[B]), dst, fl.at[l, ch])
+
+    def ffn_done(l):
+        for ch in range(2):
+            for i in range(3):
+                ffn_cp[l, ch, i].wait_send()
+            for cp in ffn_cp[l, ch, "out"]:
+                cp.wait()
+            ffn_cp[l, ch, "own"].wait()
+
+    gn_cp = {}
+
+    def gn_send(step):
+        gn_cp[step] = remote(gn, gnr.at[step], gn_s.at[step], gn_r.at[step], peer(AXES[step]))
+
+    def gn_recv(step):
+        gn_cp[step].wait()
+        gn[...] = gn[...] + gnr[step]
+        if step < 3:
+            gn_send(step + 1)
+
+    x_cp.wait()
+    for rows in row_chunks:
+        xcur[rows, :] = ab[rows, :].astype(F32)
+    cps = fwd_attention(0)
+    fwd_norm1(0, cps)
+    cps = fwd_ffn(0)
+    fwd_norm2(0, cps)
+    cps = fwd_attention(1, mid=pairs[0].share)
+    fwd_norm1(1, cps)
+    cps = fwd_ffn(1)
+    cot_cp = here(cot_hbm, ab, insem.at[1])
+    fwd_norm2(1, cps)
+
+    cot_cp.wait()
+    bwd_norm2(1, lambda rows: ab[rows, :].astype(F32))
+    groups[0].forward()
+    pairs[1].share()
+    cps = bwd_ffn(1)
+    bwd_norm1(1, cps)
+    cps = bwd_attention(1, late=groups[1].forward)
+    att_own(1)
+    groups[0].share()
+    bwd_input(1, cps)
+    groups[2].forward()
+    groups[2].sent()
+    groups[2].own.wait()
+    bwd_norm2(0, lambda rows: xcur[rows, :])
+    cps = bwd_ffn(0)
+    bwd_norm1(0, cps)
+    pairs[2].share()
+    gn_send(0)
+    cps = bwd_attention(0, late=groups[1].share)
+    bwd_input(0, cps)
+    groups[2].share()
+    igrad_cp = here(xcur, igrad_ref, igl.at[0])
+    att_partner(1)
+    groups[3].forward()
+    att_grad(1, 0)
+    att_grad(1, 1)
+    gn_recv(0)
+    groups[1].ready()
+    groups[2].ready()
+    ffn_hidden(1)
+    for i in range(4):
+        ffn_block(1, i)
+    pairs[3].share()
+    groups[3].share()
+    gn_recv(1)
+    att_own(0)
+    att_partner(0)
+    att_recv(1, 1, 0)
+    att_grad(0, 0)
+    att_grad(0, 1)
+    gn_recv(2)
+    groups[0].ready()
+    groups[3].own.wait()
+    groups[3].ready()
+    ffn_hidden(0)
+    att_recv(1, 0, 0)
+    gn_recv(3)
+    ffn_block(0, 0)
+    ffn_recv(1, 1, 0)
+    ffn_block(0, 1)
+    ffn_block(0, 2)
+    ffn_block(0, 3)
+    ffn_recv(1, 1, 1)
+    att_recv(1, 1, 1)
+    ffn_recv(1, 0, 0)
+    ffn_recv(0, 0, 0)
+    ffn_recv(0, 0, 1)
+    ffn_recv(1, 0, 1)
+    ffn_recv(0, 1, 0)
+    att_recv(1, 0, 1)
+    ffn_recv(0, 1, 1)
+    att_recv(1, 1, 2)
+    att_recv(1, 0, 2)
+    ffn_recv(1, 1, 2)
+    att_recv(0, 0, 0)
+    ffn_recv(0, 1, 2)
+    att_recv(0, 1, 0)
+    att_recv(0, 0, 1)
+    att_recv(0, 1, 1)
+    ffn_recv(0, 0, 2)
+    ffn_recv(1, 0, 2)
+    att_recv(0, 0, 2)
+    att_recv(0, 1, 2)
+
+    igrad_cp.wait()
+    for k in (0, 1, 3):
+        groups[k].sent()
+    for l in range(L):
+        att_done(l)
+        ffn_done(l)
+
+
+def fused(inputs, lengths, w_qkv, w_out, w_in, w_down, norm_gain, norm_bias, cotangent):
+    T, D = inputs.shape
+    L, _, _, E = w_qkv.shape
+    F = w_in.shape[-1]
+    W, NP, NC, FQ = T // 128, E // 128, D // 256, F // GROUP
+    R = D // DP
+    RB = 4 * R
+    vmem = pl.BlockSpec(memory_space=pltpu.VMEM)
+    smem = pl.BlockSpec(memory_space=pltpu.SMEM)
+    hbm = pl.BlockSpec(memory_space=pl.ANY)
+    V = pltpu.VMEM
+    DMA = pltpu.SemaphoreType.DMA
+    scratch = [
+        V((L, 3, D, E), BF16), V((L, E, D), BF16), V((L, 2, D, F), BF16), V((L, F, D), BF16),
+        V((L, T, D), BF16), V((L, 3, T, E), BF16), V((L, W, NP, 128, 256), BF16), V((L, T, E), BF16),
+        V((L, T, D), BF16), V((L, T, D), BF16), V((L, T, 1), F32), V((L, T, 1), F32),
+        V((T, D), F32), V((T, D), F32), V((T, D), BF16),
+        V((2, T, D), F32), V((2, T, D), F32),
+        V((T, F), BF16), V((L, 2, T, F), BF16),
+        V((2, D, 2 * T), BF16), V((2 * T, 6 * 128), BF16),
+        V((D, GROUP * T), BF16), V((D, GROUP * T), BF16),
+        V((T, D), BF16), V((T, D), BF16), V((1 + L, 8, 128), F32),
+        V((L, 2, 2, 3, RB, FQ), F32), V((L, 2, 3, RB, FQ), F32), V((L, 3, RB, FQ), F32),
+        V((L, 2, 2, 2, 2, 2, 3, R, 128), F32),
+        V((L, 2, 2, 2, 2, 3, R, 128), F32), V((L, 2, 2, 2, 3, R, 128), F32), V((L, 2, 2, 3, R, 128), F32),
+        V((4, 4 * L, D), F32),
+        DMA((L, 4)), DMA((2,)), DMA((2, NC)), DMA((2, NC)),
+        DMA((2 * L,)), DMA((2 * L,)), DMA((2 * L,)), DMA((2 * L,)), DMA((2 * L,)), DMA((2 * L,)), DMA((2 * L,)),
+        DMA((2 * L, 3)), DMA((2 * L, 3)),
+        DMA((L,)), DMA((L,)), DMA((1,)),
+        DMA((2 * L,)), DMA((2 * L,)), DMA((2 * L,)), DMA((2 * L,)), DMA((2 * L,)),
+        DMA((2,)), DMA((L, 2, 3)), DMA((L, 2, 3)), DMA((L, 2, 3)), DMA((L, 2, 3)), DMA((L, 2)),
+        DMA((L, 2, 3)), DMA((L, 2, 3)), DMA((L, 4)), DMA((L, 4)), DMA((L, 4)),
+        DMA((4,)), DMA((4,)),
+    ]
+    outs = pl.pallas_call(
+        functools.partial(kernel, T, D, E, F, L),
+        out_shape=(
+            jax.ShapeDtypeStruct((T, D), BF16),
+            jax.ShapeDtypeStruct((T, D), F32),
+            jax.ShapeDtypeStruct((L, 4, R, E), F32),
+            jax.ShapeDtypeStruct((L, 3, R, F), F32),
+            jax.ShapeDtypeStruct((4 * L, D), F32),
+            jax.ShapeDtypeStruct((2 * L, 2, 2, T, D), F32),
+            jax.ShapeDtypeStruct((2 * L, 2, T, D), F32),
+        ),
+        in_specs=[smem, hbm, hbm, vmem, vmem, hbm, hbm, hbm, hbm],
+        out_specs=(vmem, hbm, hbm, hbm, vmem, hbm, hbm),
+        scratch_shapes=scratch,
+        compiler_params=pltpu.CompilerParams(collective_id=0, has_side_effects=True, vmem_limit_bytes=63 * 2**20),
+        name="encoder",
+    )(lengths, inputs, cotangent, norm_gain, norm_bias, w_qkv, w_out, w_in, w_down)
+    encoded, input_grad, oatt, offn, gn, _, _ = outs
+    mine = lax.dynamic_slice_in_dim(gn.reshape(2, L, 2, D), lax.axis_index("dp") * R, R, axis=3)
+    return (
+        encoded,
+        input_grad,
+        oatt[:, :3],
+        jnp.swapaxes(oatt[:, 3], 1, 2),
+        offn[:, :2],
+        jnp.swapaxes(offn[:, 2], 1, 2),
+        mine[0],
+        mine[1],
+    )
 
 
 def normalize(values, gain_vec, shift_vec):
@@ -216,7 +1028,7 @@
 
 def solution(mesh):
     return jax.shard_map(
-        body,
+        fused if mesh.shape["dp"] == DP and mesh.shape["tensor"] == 2 else body,
         mesh=mesh,
         in_specs=(
             P("dp", None),

time: 1580 us -> 214 us (0.14)
  waiting for transfers between devices: 1310 us -> 0 us
  Pallas kernels: 0 us -> 203 us
  local copies, waits for them, and re-layouts: 109 us -> 10.1 us
  matrix products: 76.8 us -> 0 us
  other arithmetic: 50.4 us -> 0 us
  between operations: 16.7 us -> 0.68 us
    unnamed x16 -> x0, waiting for transfers between devices: 1160 us -> none
    pallas_call x0 -> x1, Pallas kernels: none -> 203 us  [fused(): pl.pallas_call(functools.partial(kernel, T, D, E, F, L), out_shape=(jax.S...]
    psum x8 -> x0, waiting for transfers between devices: 155 us -> none  [the longest x2 41.6 us: layer_forward(): lax.psum(jnp.dot(mixed_heads, out_weight, preferred_element_type=jnp.floa...]
    dot_general x36 -> x0, matrix products: 76.8 us -> none  [the longest x2 9.87 us: layer_forward(): jnp.dot(gated_low, down_weight, preferred_element_type=jnp.float32)]
    another operation x16 -> x0, local copies, waits for them, and re-layouts: 66.8 us -> none  [the longest x4 62.5 us: body(): jnp.stack([pieces[index][member] for index in range(layers)])]
    another operation x14 -> x0, other arithmetic: 30.1 us -> none  [the longest x10 21.7 us: body(): jnp.stack([pieces[index][member] for index in range(layers)])]
    unnamed x243 -> x8, local copies, waits for them, and re-layouts: 30.6 us -> 1.64 us
    reduce_sum x18 -> x0, other arithmetic: 16.8 us -> none  [the longest x8 8.18 us: normalize(): center = values - jnp.mean(values, -1, keepdims=True)]
  transfers between devices with their start and end apart: 12 -> 0, of which waited for: 12 -> 0; matrix products, arithmetic and copies ran while one was open for 8% -> 0% of each run, Pallas kernels for 0% -> 0%
where the time goes in v2:
time: 214 us
  Pallas kernels  203 us (95%)
  local copies, waits for them, and re-layouts  10.1 us (5%)
    pallas_call x1, Pallas kernels, fused(): pl.pallas_call(functools.partial(kernel, T, D, E, F, L), out_shape=(jax.S...  203 us

profile of v2, /device:TPU:0, one launch (start us, length us, event | category | flops | bytes accessed | tf_op | source)
XLA Modules:
  0.0 213.5 jit_solution(1069356205936195259)
XLA Ops:
  0.6 202.8 %encoder.1 = (bf16[256,768]{1,0:T(8,128)(2,1)}, f32[256,768]{1,0:T(8,128)}, f32[2,4,48,384]{3,2,1,0:T(8,128)}, f32[2,3,48,1536]{3,2,1,0:T(8,128)}, f32[8,768]{1,...) custom-call(s32[2]{0:T(128)} %len_ref.1, bf16[256,768]{1,0:T(8,128)(2,1)} %x_hbm.1, ...), custom_call_target="tpu_custom_call" | custom-call | tf_op jit(solution)/shard_map/encoder/pallas_call | solution.py:795
  203.4 0.0 copy-start.2
  203.4 0.0 copy-start.1
  203.4 0.0 copy-start
  203.5 1.9 slice.18
  205.4 1.6 slice_bitcast_fusion.1
  206.9 2.4 %slice.20 = f32[2,2,48,1536]{3,2,1,0:T(8,128)} slice(f32[2,3,48,1536]{3,2,1,0:T(8,128)} %get-tuple-element.16), slice={[0:2], [0:2], [0:48], [0:1536]} | slice | bytes 2359296 | tf_op jit(solution)/shard_map/slice | solution.py:819
  209.3 1.9 slice_bitcast_fusion
  211.2 0.0 copy-done.2
  211.2 0.7 dynamic-slice_bitcast_fusion
  211.9 0.0 copy-done.1
  211.9 0.7 copy.19
  212.7 0.0 copy-done
  212.7 0.9 copy.20
  (1 shorter events, 0.0 us)
Async XLA Ops:
  203.4 7.8 %copy-start.2 = (f32[8,768]{1,0:T(8,128)S(1)}, f32[8,768]{1,0:T(8,128)}, u32[]{:S(2)}) copy-start(f32[8,768]{1,0:T(8,128)} %get-tuple-element.17) | copy-start | bytes 73732
  203.4 8.5 %copy-start.1 = (bf16[256,768]{1,0:T(8,128)(2,1)S(1)}, bf16[256,768]{1,0:T(8,128)(2,1)}, u32[]{:S(2)}) copy-start(bf16[256,768]{1,0:T(8,128)(2,1)} %get-tuple-element.28) | copy-start | bytes 1179652
  203.4 9.2 %copy-start = (f32[256,768]{1,0:T(8,128)S(1)}, f32[256,768]{1,0:T(8,128)}, u32[]{:S(2)}) copy-start(f32[256,768]{1,0:T(8,128)} %get-tuple-element.29) | copy-start | bytes 2359300
